TPU v7x, 256 devices: a whole 4x4x8 slice. The times are simulated.
256 devices in a mesh: term: 16 (over y, x_lo, core), topic: 16 (over x_hi, z).
Axes of the slice: x: 4 (x_hi: 2, x_lo: 2; x = x_hi * 2 + x_lo), y: 4, z: 8, core: 2. Of those that a mesh axis runs over, the one named last changes fastest.
Arguments:
- factor: bfloat16 [131072, 2048], P('term', 'topic'), may hold values from 1e-06 to 0.05, as said below
- tile_values: bfloat16 [131072, 128], P('term'), may hold values from 0.049804688 to 1
- tile_docs: int32 [16, 128], P('term'), may hold values from 0 to 255, as said below
- codes: float32 [2048, 256], P('topic', 'term'), may hold values from 0.1 to 2
- gram_stat: float32 [2048, 2048], P('topic', 'term'), may hold values from 0 to 4
- data_stat: float32 [131072, 2048], P('term', 'topic'), may hold values from 0 to 0.4
Outputs:
- codes_out: float32 [2048, 256], P('topic', 'term')
- gram_new: float32 [2048, 2048], P('topic', 'term')
- data_new: float32 [131072, 2048], P('term', 'topic')
Inputs may be any that keep to these rules, and one draw needn't show every extreme that they name: `tile_docs`: each row lists 128 different document numbers. `factor`: positive entries.
All inputs are finite; a program needn't handle non-finite values.
Results may differ from a plain program's by a relative error of at most 0.0003.
Values may be sent and summed in bfloat16 or wider, within the bound.
A program may use at most 128 MiB of HBM per device.

v0:
```python
import jax
import jax.numpy as jnp
from jax import lax
from jax.sharding import PartitionSpec as P

ITERS = 3


EPSILON = 1e-06
DECAY = 0.5


def contract_rows(left, right):
    return lax.dot_general(
        left, right, (((0,), (0,)), ((), ())), preferred_element_type=jnp.float32
    )


def apply_gram(gram_rows, current):
    return jnp.dot(
        gram_rows,
        lax.all_gather(current, "topic", axis=0, tiled=True),
        precision=lax.Precision.HIGHEST,
        preferred_element_type=jnp.float32,
    )


def per_device(factor, tile_values, tile_docs, codes, gram_stat, data_stat):
    term_count = lax.axis_size("term")
    documents = codes.shape[1] * term_count
    onehot = (tile_docs[0][:, None] == jnp.arange(documents, dtype=jnp.int32)[None, :]).astype(
        jnp.bfloat16
    )
    batch = jnp.dot(tile_values, onehot, preferred_element_type=jnp.float32).astype(jnp.bfloat16)
    partial_data = contract_rows(factor, batch)
    data_share = lax.psum_scatter(partial_data, "term", scatter_dimension=1, tiled=True)
    row_block = lax.all_to_all(factor, "topic", split_axis=0, concat_axis=1, tiled=True)
    gram_part = lax.psum_scatter(
        contract_rows(row_block, row_block), "topic", scatter_dimension=0, tiled=True
    )
    gram_rows = lax.psum(gram_part, "term")
    current = codes
    for update in range(ITERS):
        current = current * data_share / (apply_gram(gram_rows, current) + EPSILON)
    outer = lax.dot_general(
        current,
        lax.all_gather(current, "topic", axis=0, tiled=True),
        (((1,), (1,)), ((), ())),
        precision=lax.Precision.HIGHEST,
        preferred_element_type=jnp.float32,
    )
    outer_share = lax.psum_scatter(outer, "term", scatter_dimension=1, tiled=True)
    gram_new = DECAY * gram_stat + outer_share / documents
    code_row = lax.all_gather(current, "term", axis=1, tiled=True)
    widened = batch.astype(jnp.float32)
    product = lax.dot_general(
        widened,
        code_row,
        (((1,), (1,)), ((), ())),
        precision=lax.Precision.HIGHEST,
        preferred_element_type=jnp.float32,
    )
    data_new = DECAY * data_stat + product / documents
    return (current, gram_new, data_new)


def solution(mesh):
    placed = (
        P("term", "topic"),
        P("term", None),
        P("term", None),
        P("topic", "term"),
        P("topic", "term"),
        P("term", "topic"),
    )
    return jax.shard_map(
        per_device,
        mesh=mesh,
        in_specs=placed,
        out_specs=(P("topic", "term"), P("topic", "term"), P("term", "topic")),
        check_vma=False,
    )
```

profile of v0, /device:TPU:1, one launch (start us, length us, event | category | flops | bytes accessed | tf_op | source)
XLA Modules:
  0.0 743.5 jit_solution(4926466583788297167)
XLA Ops:
  7.2 0.0 copy-start
  7.2 0.0 reduce-scatter.6.cloned.1.call-start
  7.2 60.8 %all_to_all.19 = bf16[16,512,128]{2,1,0:T(8,128)(2,1)} all-to-all(bf16[16,512,128]{2,1,0:T(8,128)(2,1)} %bitcast.21), channel_id=1, replica_groups=mesh['term'=16,'topic'=16] {'topic'}, dimensions={0} | all-to-all | bytes 4194304 | tf_op jit(solution)/shard_map/all_to_all | solution.py:37
  68.0 3.9 copy.9
  71.9 12.5 %fusion.7 = f32[2048,2048]{1,0:T(8,128)} fusion(bf16[512,2048]{0,1:T(8,128)(2,1)} %bitcast.23), kind=kOutput, calls=%fused_computation.14 | convolution fusion | flops 4294967296 | bytes 18874368 | tf_op jit(solution)/shard_map/dot_general | solution.py:14
  84.4 0.0 copy-start.6
  84.4 0.0 reduce-scatter.6.cloned.1.call-update
  84.4 0.0 reduce-scatter.4.cloned.1.call-start
  84.5 0.0 copy-start.2
  84.5 0.0 copy-done
  84.5 0.6 copy-done.6
  85.1 1.4 convolution_convert_fusion
  86.4 0.0 copy-start.1
  86.4 1.9 copy-done.1
  88.4 0.0 copy-done.2
  88.4 0.0 copy-start.5
  88.4 1.9 convolution_bitcast_fusion
  90.3 0.0 reduce-scatter.4.cloned.1.call-update
  90.3 0.0 all-reduce.2.cloned.1.call-start
  90.3 278.5 %reduce-scatter.6.cloned.1.call-done = f32[128,2048]{1,0:T(8,128)} async-done(((f32[2048,2048]{1,0:T(8,128)}), f32[128,2048]{1,0:T(8,128)}) %reduce-scatter.6.cloned.1.call-update) | async-done | bytes 1048592 | tf_op jit(solution)/shard_map/reduce_scatter | solution.py:38
  368.8 0.0 all-reduce.2.cloned.1.call-update
  368.8 0.0 reduce-scatter.8.cloned.1.call-start
  368.9 0.0 copy-done.5
  368.9 30.5 %all_gather.15 = f32[2048,16]{0,1:T(8,128)S(1)} all-gather(f32[128,16]{0,1:T(8,128)S(1)} %copy-done.5), channel_id=1, replica_groups=mesh['term'=16,'topic'=16] {'topic'}, dimensions={0}, use_global_device_ids=true | all-gather | bytes 139264 | tf_op jit(solution)/shard_map/all_gather | solution.py:22
  399.4 30.0 %reduce-scatter.4.cloned.1.call-done = f32[128,16]{0,1:T(8,128)} async-done(((f32[128,256]{0,1:T(8,128)}), f32[128,16]{0,1:T(8,128)}) %reduce-scatter.4.cloned.1.call-update) | async-done | bytes 8208 | tf_op jit(solution)/shard_map/reduce_scatter | solution.py:36
  429.4 128.6 %all-reduce.2.cloned.1.call-done = f32[128,2048]{1,0:T(8,128)} async-done(((f32[128,2048]{1,0:T(8,128)}), f32[128,2048]{1,0:T(8,128)}) %all-reduce.2.cloned.1.call-update) | async-done | bytes 1048592 | tf_op jit(solution)/shard_map/psum | solution.py:41
  558.0 2.2 fusion.3
  560.1 34.7 %all_gather.16 = f32[2048,16]{0,1:T(8,128)S(1)} all-gather(f32[128,16]{0,1:T(8,128)S(1)} %fusion.3), channel_id=1, replica_groups=mesh['term'=16,'topic'=16] {'topic'}, dimensions={0}, use_global_device_ids=true | all-gather | bytes 139264 | tf_op jit(solution)/shard_map/all_gather | solution.py:22
  594.9 2.2 fusion.2
  597.0 29.3 %all_gather.17 = f32[2048,16]{0,1:T(8,128)S(1)} all-gather(f32[128,16]{0,1:T(8,128)S(1)} %fusion.2), channel_id=1, replica_groups=mesh['term'=16,'topic'=16] {'topic'}, dimensions={0}, use_global_device_ids=true | all-gather | bytes 139264 | tf_op jit(solution)/shard_map/all_gather | solution.py:22
  626.3 2.2 fusion.1
  628.5 0.0 copy-start.3
  628.5 31.4 %all_gather.18 = f32[2048,16]{0,1:T(8,128)S(1)} all-gather(f32[128,16]{0,1:T(8,128)S(1)} %fusion.1), channel_id=1, replica_groups=mesh['term'=16,'topic'=16] {'topic'}, dimensions={0}, use_global_device_ids=true | all-gather | bytes 139264 | tf_op jit(solution)/shard_map/all_gather | solution.py:47
  659.9 2.0 fusion.8
  661.9 0.0 reduce-scatter.8.cloned.1.call-update
  661.9 38.5 %all_gather.19 = f32[128,256]{0,1:T(8,128)S(1)} all-gather(f32[128,16]{0,1:T(8,128)S(1)} %fusion.1), channel_id=1, replica_groups=mesh['term'=16,'topic'=16] {'term'}, dimensions={1}, use_global_device_ids=true | all-gather | bytes 139264 | tf_op jit(solution)/shard_map/all_gather | solution.py:54
  700.4 0.0 copy-start.4
  700.4 10.0 %fusion = f32[8192,128]{1,0:T(8,128)} fusion(bf16[256,8192]{1,0:T(8,128)(2,1)} %copy-done.1, f32[128,256]{0,1:T(8,128)S(1)} %all_gather.19, f32[8192,128]{1,0:T(8,128)} %param.11), kind=kOutput, calls=%fused_computation.2 | convolution fusion | flops 3224371200 | bytes 12713984 | tf_op jit(solution)/shard_map/dot_general | solution.py:56
  710.4 0.0 copy-done.3
  710.4 25.0 %reduce-scatter.8.cloned.1.call-done = f32[128,128]{1,0:T(8,128)} async-done(((f32[128,2048]{1,0:T(8,128)}), f32[128,128]{1,0:T(8,128)}) %reduce-scatter.8.cloned.1.call-update) | async-done | bytes 65552 | tf_op jit(solution)/shard_map/reduce_scatter | solution.py:52
  735.5 0.0 copy-done.4
  735.5 1.5 multiply_add_fusion
Async XLA Ops:
  7.2 77.3 %copy-start = (bf16[8192,128]{1,0:T(8,128)(2,1)S(1)}, bf16[8192,128]{1,0:T(8,128)(2,1)}, u32[]{:S(2)}) copy-start(bf16[8192,128]{1,0:T(8,128)(2,1)} %param.7) | copy-start | bytes 6291460
  7.2 361.6 %reduce-scatter.6.cloned.1.call-start = ((), (), s32[]{:S(2)}) async-start(), calls=%async_computation.5 | async-start | bytes 17825792 | tf_op jit(solution)/shard_map/reduce_scatter | solution.py:38
  84.4 0.7 copy-start.6
  84.4 344.9 %reduce-scatter.4.cloned.1.call-start = ((), (), s32[]{:S(2)}) async-start(), calls=%async_computation.4 | async-start | bytes 139264 | tf_op jit(solution)/shard_map/reduce_scatter | solution.py:36
  84.5 3.9 copy-start.2
  86.4 1.9 copy-start.1
  88.4 280.5 %copy-start.5 = (f32[128,16]{0,1:T(8,128)S(1)}, f32[128,16]{0,1:T(8,128)}, u32[]{:S(2)}) copy-start(f32[128,16]{0,1:T(8,128)} %param.9) | copy-start | bytes 24580
  90.3 467.7 %all-reduce.2.cloned.1.call-start = ((), (), s32[]{:S(2)}) async-start(), calls=%async_computation.6 | async-start | bytes 2097152 | tf_op jit(solution)/shard_map/psum | solution.py:41
  368.8 366.6 %reduce-scatter.8.cloned.1.call-start = ((), (), s32[]{:S(2)}) async-start(), calls=%async_computation.7 | async-start | bytes 1114112 | tf_op jit(solution)/shard_map/reduce_scatter | solution.py:52
  628.5 81.9 %copy-start.3 = (f32[128,16]{0,1:T(8,128)}, f32[128,16]{0,1:T(8,128)S(1)}, u32[]{:S(2)}) copy-start(f32[128,16]{0,1:T(8,128)S(1)} %fusion.1) | copy-start | bytes 24580
  700.4 35.1 %copy-start.4 = (f32[128,128]{1,0:T(8,128)S(1)}, f32[128,128]{1,0:T(8,128)}, u32[]{:S(2)}) copy-start(f32[128,128]{1,0:T(8,128)} %param.10) | copy-start | bytes 196612
Sparse Core Ops, SparseCore 0:
  84.5 284.2 reduce-scatter.5
  371.9 57.4 reduce-scatter.3
  432.2 125.7 all-reduce.1
  662.0 73.4 reduce-scatter.7
where the time goes:
time: 746 us; the launch traced here: 743 us
  waiting for transfers between devices  462 us (62%)
  blocking collectives  225 us (30%)
  matrix products  34.3 us (5%)
  between operations  13.8 us (2%)
    reduce_scatter x1, waiting for transfers between devices, per_device(): lax.psum_scatter(contract_rows(row_block, row_block), 'topic', scatter_di...  278 us
    psum x1, waiting for transfers between devices, per_device(): gram_rows = lax.psum(gram_part, 'term')  129 us
    all_gather x3, blocking collectives, apply_gram(): lax.all_gather(current, 'topic', axis=0, tiled=True)  94.5 us
    all_to_all x1, blocking collectives, per_device(): lax.all_to_all(factor, 'topic', split_axis=0, concat_axis=1, tiled=True)  60.8 us
    all_gather x1, blocking collectives, per_device(): code_row = lax.all_gather(current, 'term', axis=1, tiled=True)  38.5 us
    all_gather x1, blocking collectives, per_device(): lax.all_gather(current, 'topic', axis=0, tiled=True)  31.4 us
    reduce_scatter x1, waiting for transfers between devices, per_device(): lax.psum_scatter(partial_data, 'term', scatter_dimension=1, tiled=True)  30 us
    reduce_scatter x1, waiting for transfers between devices, per_device(): lax.psum_scatter(outer, 'term', scatter_dimension=1, tiled=True)  25 us
  transfers between devices with their start and end apart: 4, of which 4 were waited for; matrix products, arithmetic and copies ran while one was open for 2% of the time, Pallas kernels for 0%

commit v1 on v0

v1 whole, which is shorter than its diff:
```python
import functools

import jax
import jax.numpy as jnp
from jax import lax
from jax.experimental import pallas as pl
from jax.experimental.pallas import tpu as pltpu
from jax.sharding import PartitionSpec as P

ITERS = 3
EPSILON = 1e-06
DECAY = 0.5
MESH = pl.DeviceIdType.MESH
BF = jnp.bfloat16
F32 = jnp.float32


def split2(value):
    high = value.astype(BF)
    return high, (value - high.astype(F32)).astype(BF)


def dot(left, right):
    return jnp.dot(left, right, preferred_element_type=F32)


def codes_kernel(
    n, factor, tiles, docs, codes, gram_stat,
    codes_out, row_out, gram_out,
    factor_v, tiles_v, xx, xt, own, outgoing, incoming, across, zin,
    gcol, gsend, cbuf, csend, dsend, drecv, fsend, arow, brow,
    local_sem, a2a_send, a2a_recv, core_send, core_recv, y_send, y_recv,
    x_send, x_recv, z_send, z_recv, g_send, g_recv, c_send, c_recv,
    d_send, d_recv, fa_send, fa_recv, fb_send, fb_recv,
):
    rows, topics = factor.shape
    piece = rows // n
    block = codes.shape[0]
    half = n // 2
    ny = n // 4
    d = lax.axis_index("term")
    t = lax.axis_index("topic")
    core = d % 2
    xlo = (d // 2) % 2
    y = d // 4
    sibling = d + 1 - 2 * core
    across_d = d + 2 - 4 * xlo

    barrier = pltpu.get_barrier_semaphore()

    def greet(s, carry):
        pl.semaphore_signal(barrier, 1, device_id={"topic": (t + s) % n}, device_id_type=MESH)
        pl.semaphore_signal(barrier, 1, device_id={"term": (d + s) % n}, device_id_type=MESH)
        return carry

    lax.fori_loop(1, n, greet, 0)

    def greet_senders(s, carry):
        @pl.when((s != d) | (t != d))
        def _():
            pl.semaphore_signal(barrier, 1, device_id={"term": s, "topic": d}, device_id_type=MESH)
        return carry

    lax.fori_loop(0, n, greet_senders, 0)
    load_factor = pltpu.make_async_copy(factor, factor_v, local_sem.at[0])
    load_tiles = pltpu.make_async_copy(tiles, tiles_v, local_sem.at[1])
    load_own = pltpu.make_async_copy(
        factor.at[pl.ds(t * piece, piece)], xx.at[t, pl.ds(core * piece, piece)], a2a_recv.at[t]
    )
    load_own.start()
    load_factor.start()
    load_tiles.start()

    @pl.when(t == d)
    def _():
        pl.semaphore_wait(barrier, 3 * n - 3)

    @pl.when(t != d)
    def _():
        pl.semaphore_wait(barrier, 3 * n - 2)

    def send_piece(s, carry):
        p = (t + s) % n
        pltpu.make_async_remote_copy(
            factor.at[pl.ds(p * piece, piece)],
            xx.at[t, pl.ds(core * piece, piece)],
            a2a_send,
            a2a_recv.at[t],
            device_id={"topic": p},
            device_id_type=MESH,
        ).start()
        return carry

    lax.fori_loop(1, n, send_piece, 0)

    load_factor.wait()
    load_tiles.wait()
    share = jnp.zeros((tiles.shape[1], topics), F32)
    for s in range(n):
        part = tiles_v[s * piece:(s + 1) * piece, :]
        share = share + lax.dot_general(
            part, factor_v[s * piece:(s + 1) * piece, :], (((0,), (0,)), ((), ())),
            preferred_element_type=F32,
        )
    onehot = (
        lax.broadcasted_iota(jnp.int32, (n * block, tiles.shape[1]), 0) == docs[...]
    ).astype(F32).astype(BF)
    high, middle = split2(share)
    low = (share - high.astype(F32) - middle.astype(F32)).astype(BF)
    spread = dot(onehot, high) + dot(onehot, middle) + dot(onehot, low)
    dsend[...] = spread.reshape(n, block, topics)

    def send_share(s, carry):
        target = (d + s) % n
        pltpu.make_async_remote_copy(
            dsend.at[target], drecv.at[d], d_send, d_recv,
            device_id={"term": target}, device_id_type=MESH,
        ).start()
        return carry

    lax.fori_loop(1, n, send_share, 0)
    drecv[d] = dsend[d]

    def place(p, q):
        k = (p + q) % n
        e1 = (p + n - k // 2 - core) % n
        swap = (e1 + half - 1 + core) // n
        i = p + swap * (q - p)
        j = q + swap * (p - q)
        e = (i + n - k // 2 - core) % n
        return k // 4, (k // 2) % 2, e, i, j

    def pair_count(m):
        return (m - (m + core) % 2 + 2) // 2

    def forward(p):
        return pltpu.make_async_remote_copy(
            xx.at[p, pl.ds(core * piece, piece)],
            xx.at[p, pl.ds(core * piece, piece)],
            core_send,
            core_recv.at[p],
            device_id={"term": sibling},
            device_id_type=MESH,
        )

    def arrive(m, carry):
        p = (t + n - m) % n
        mine = xx.at[p, pl.ds(core * piece, piece)]
        pltpu.make_async_copy(mine, mine, a2a_recv.at[p]).wait()
        forward(p).start()
        theirs = xx.at[p, pl.ds((1 - core) * piece, piece)]
        pltpu.make_async_copy(theirs, theirs, core_recv.at[p]).wait()
        xt[p] = xx[p].T

        def pair(s, carry):
            q = (t + n - ((m + core) % 2 + 2 * s)) % n
            y2, x2, e, i, j = place(p, q)
            tile = dot(xt[i], xx[j])

            @pl.when(y2 == y)
            def _():
                own[x2, e] = tile

            @pl.when(y2 != y)
            def _():
                outgoing[y2, x2, e] = tile.astype(BF)
                pltpu.make_async_remote_copy(
                    outgoing.at[y2, x2, e], incoming.at[y, x2, e], y_send, y_recv.at[y, x2, e],
                    device_id={"term": y2 * 4 + xlo * 2 + core}, device_id_type=MESH,
                ).start()

            return carry

        lax.fori_loop(0, pair_count(m), pair, 0)
        return carry

    lax.fori_loop(0, n, arrive, 0)

    def walk(x_want, body):
        def outer_loop(m, carry):
            p = (t + n - m) % n

            def inner(s, carry):
                q = (t + n - ((m + core) % 2 + 2 * s)) % n
                y2, x2, e, i, j = place(p, q)

                @pl.when((y2 == y) & (x2 == x_want))
                def _():
                    body(e, i, j)

                return carry

            lax.fori_loop(0, pair_count(m), inner, 0)
            return carry

        lax.fori_loop(0, n, outer_loop, 0)

    def sum_y(x2, e):
        total = own[x2, e]
        for s in range(1, ny):
            y2 = (y + s) % ny
            got = incoming.at[y2, x2, e]
            pltpu.make_async_copy(got, got, y_recv.at[y2, x2, e]).wait()
            total = total + incoming[y2, x2, e].astype(F32)
        return total

    def send_across(e, i, j):
        own[1 - xlo, e] = sum_y(1 - xlo, e)
        pltpu.make_async_remote_copy(
            own.at[1 - xlo, e], across.at[e], x_send, x_recv.at[e],
            device_id={"term": across_d}, device_id_type=MESH,
        ).start()

    def send_tile(e, target):
        @pl.when(target == t)
        def _():
            zin[t] = own[xlo, e]

        @pl.when(target != t)
        def _():
            pltpu.make_async_remote_copy(
                own.at[xlo, e], zin.at[t], z_send, z_recv,
                device_id={"topic": target}, device_id_type=MESH,
            ).start()

    def send_both(e, i, j):
        total = sum_y(xlo, e)
        pltpu.make_async_copy(across.at[e], across.at[e], x_recv.at[e]).wait()
        own[xlo, e] = total + across[e]
        send_tile(e, i)

        @pl.when(i != j)
        def _():
            send_tile(e, j)

    walk(1 - xlo, send_across)
    walk(xlo, send_both)

    zparts = zin.at[pl.ds(0, n - 1)]
    pltpu.make_async_copy(zparts, zparts, z_recv).wait()
    total = zin[0]
    for s in range(1, n):
        total = total + zin[s]
    first_role = (t + n - d // 2 - core) % n

    @pl.when(first_role <= half - core)
    def _():
        high, middle = split2(total.T)
        gsend[:, :topics] = high
        gsend[:, topics:] = middle

    @pl.when(first_role > half - core)
    def _():
        high, middle = split2(total)
        gsend[:, :topics] = high
        gsend[:, topics:] = middle

    position = (d + n - t) % n

    def send_gram(s, carry):
        pltpu.make_async_remote_copy(
            gsend, gcol.at[pl.ds(position * topics, topics)], g_send, g_recv,
            device_id={"term": (d + s) % n}, device_id_type=MESH,
        ).start()
        return carry

    lax.fori_loop(1, n, send_gram, 0)
    gcol[pl.ds(position * topics, topics), :] = gsend[...]

    dparts = drecv.at[pl.ds(0, n - 1)]
    pltpu.make_async_copy(dparts, dparts, d_recv).wait()
    data = drecv[0]
    for s in range(1, n):
        data = data + drecv[s]

    current = codes[...]
    for step in range(ITERS):
        high, middle = split2(current)
        csend[step, :block, :] = high
        csend[step, block:, :] = middle

        def send_codes(s, carry):
            pltpu.make_async_remote_copy(
                csend.at[step],
                cbuf.at[step, :, pl.ds(pl.multiple_of(t * topics, topics), topics)],
                c_send.at[step],
                c_recv.at[step],
                device_id={"topic": (t + s) % n},
                device_id_type=MESH,
            ).start()
            return carry

        lax.fori_loop(1, n, send_codes, 0)
        cbuf[step, :, pl.ds(pl.multiple_of(t * topics, topics), topics)] = csend[step]
        if step == 0:
            gparts = gcol.at[pl.ds(0, (n - 1) * topics)]
            pltpu.make_async_copy(gparts, gparts, g_recv).wait()
        cparts = cbuf.at[step, :, pl.ds(0, (n - 1) * topics)]
        pltpu.make_async_copy(cparts, cparts, c_recv.at[step]).wait()
        product = dot(cbuf[step], gcol[...])
        applied = product[:, :topics] + product[:, topics:]
        applied = applied[:block] + applied[block:]
        current = current * data / (applied + EPSILON)

    codes_out[...] = current
    fsend[...] = current

    def send_row(s, carry):
        pltpu.make_async_remote_copy(
            fsend, arow.at[d], fa_send, fa_recv,
            device_id={"term": (d + s) % n}, device_id_type=MESH,
        ).start()
        return carry

    lax.fori_loop(1, n, send_row, 0)

    def send_column(s, carry):
        target = (t + s) % n

        @pl.when((t != d) | (target != t))
        def _():
            pltpu.make_async_remote_copy(
                fsend, brow.at[d], fb_send, fb_recv,
                device_id={"term": t, "topic": target}, device_id_type=MESH,
            ).start()

        return carry

    lax.fori_loop(0, n, send_column, 0)
    arow[d] = current
    aparts = arow.at[pl.ds(0, n - 1)]
    pltpu.make_async_copy(aparts, aparts, fa_recv).wait()
    whole = arow[...].reshape(n * block, topics)
    row_out[...] = whole

    @pl.when(t == d)
    def _():
        brow[d] = current
        bparts = brow.at[pl.ds(0, n - 1)]
        pltpu.make_async_copy(bparts, bparts, fb_recv).wait()
        pltpu.make_async_copy(bparts, bparts, fb_send).wait()

    @pl.when(t != d)
    def _():
        pltpu.make_async_copy(brow, brow, fb_recv).wait()
        pltpu.make_async_copy(brow, brow, fb_send).wait()

    a_high, a_middle = split2(whole.T)
    b_high, b_middle = split2(brow[...].reshape(n * block, topics))
    outer = dot(a_high, b_high) + (dot(a_high, b_middle) + dot(a_middle, b_high))
    gram_out[...] = DECAY * gram_stat[...] + outer / (n * block)

    sent = factor.at[pl.ds(0, rows - piece)]
    pltpu.make_async_copy(sent, sent, a2a_send).wait()
    pltpu.make_async_copy(factor, factor, core_send).wait()
    for c in range(2):
        @pl.when(core == c)
        def _():
            if ny > 1:
                y_part = outgoing.at[pl.ds(0, ny - 1), :, pl.ds(0, half + 1 - c)]
                pltpu.make_async_copy(y_part, y_part, y_send).wait()
            x_part = across.at[pl.ds(0, half + 1 - c)]
            pltpu.make_async_copy(x_part, x_part, x_send).wait()

    pltpu.make_async_copy(zparts, zparts, z_send).wait()
    pltpu.make_async_copy(gparts, gparts, g_send).wait()
    pltpu.make_async_copy(dparts, dparts, d_send).wait()
    for step in range(ITERS):
        cparts = cbuf.at[step, :, pl.ds(0, (n - 1) * topics)]
        pltpu.make_async_copy(cparts, cparts, c_send.at[step]).wait()
    pltpu.make_async_copy(aparts, aparts, fa_send).wait()


def statistic_kernel(tiles, docs, row, stat, out, weights):
    topics = stat.shape[1]

    @pl.when(pl.program_id(0) == 0)
    def _():
        count = row.shape[0]
        onehot = (
            lax.broadcasted_iota(jnp.int32, (count, docs.shape[1]), 0) == docs[...]
        ).astype(F32).T.astype(BF)
        high, middle = split2(row[...])
        weights[:, :topics] = dot(onehot, high).astype(BF)
        weights[:, topics:] = dot(onehot, middle).astype(BF)

    product = dot(tiles[...], weights[...])
    product = product[:, :topics] + product[:, topics:]
    out[...] = DECAY * stat[...] + product * (1.0 / row.shape[0])


def per_device(n, factor, tile_values, tile_docs, codes, gram_stat, data_stat):
    rows, topics = factor.shape
    width = tile_values.shape[1]
    block = codes.shape[1]
    piece = rows // n
    half = n // 2
    ny = n // 4
    anywhere = pl.BlockSpec(memory_space=pl.ANY)
    vmem = pl.BlockSpec(memory_space=pltpu.VMEM)
    dma = pltpu.SemaphoreType.DMA
    codes_t, row, gram_new = pl.pallas_call(
        functools.partial(codes_kernel, n),
        out_shape=(
            jax.ShapeDtypeStruct((block, topics), F32),
            jax.ShapeDtypeStruct((n * block, topics), F32),
            jax.ShapeDtypeStruct((topics, topics), F32),
        ),
        in_specs=[anywhere, anywhere, vmem, vmem, vmem],
        out_specs=(vmem, vmem, vmem),
        scratch_shapes=[
            pltpu.VMEM((rows, topics), BF),
            pltpu.VMEM((rows, width), BF),
            pltpu.VMEM((n, 2 * piece, topics), BF),
            pltpu.VMEM((n, topics, 2 * piece), BF),
            pltpu.VMEM((2, half + 1, topics, topics), F32),
            pltpu.VMEM((ny, 2, half + 1, topics, topics), BF),
            pltpu.VMEM((ny, 2, half + 1, topics, topics), BF),
            pltpu.VMEM((half + 1, topics, topics), F32),
            pltpu.VMEM((n, topics, topics), F32),
            pltpu.VMEM((n * topics, 2 * topics), BF),
            pltpu.VMEM((topics, 2 * topics), BF),
            pltpu.VMEM((ITERS, 2 * block, n * topics), BF),
            pltpu.VMEM((ITERS, 2 * block, topics), BF),
            pltpu.VMEM((n, block, topics), F32),
            pltpu.VMEM((n, block, topics), F32),
            pltpu.VMEM((block, topics), F32),
            pltpu.VMEM((n, block, topics), F32),
            pltpu.VMEM((n, block, topics), F32),
            dma((2,)), dma, dma((n,)), dma, dma((n,)), dma, dma((ny, 2, half + 1)),
            dma, dma((half + 1,)), dma, dma, dma, dma, dma((ITERS,)), dma((ITERS,)),
            dma, dma, dma, dma, dma, dma,
        ],
        compiler_params=pltpu.CompilerParams(
            collective_id=0, has_side_effects=True, vmem_limit_bytes=48 * 1024 * 1024
        ),
        name="codes",
    )(factor, tile_values, tile_docs, codes.T, gram_stat)
    step = rows // 8
    data_new = pl.pallas_call(
        statistic_kernel,
        grid=(8,),
        out_shape=jax.ShapeDtypeStruct((rows, topics), F32),
        in_specs=[
            pl.BlockSpec((step, width), lambda i: (i, 0)),
            pl.BlockSpec((1, width), lambda i: (0, 0)),
            pl.BlockSpec((n * block, topics), lambda i: (0, 0)),
            pl.BlockSpec((step, topics), lambda i: (i, 0)),
        ],
        out_specs=pl.BlockSpec((step, topics), lambda i: (i, 0)),
        scratch_shapes=[pltpu.VMEM((width, 2 * topics), BF)],
        compiler_params=pltpu.CompilerParams(vmem_limit_bytes=32 * 1024 * 1024),
        name="statistic",
    )(tile_values, tile_docs, row, data_stat)
    return codes_t.T, gram_new, data_new


def solution(mesh):
    placed = (
        P("term", "topic"),
        P("term", None),
        P("term", None),
        P("topic", "term"),
        P("topic", "term"),
        P("term", "topic"),
    )
    return jax.shard_map(
        functools.partial(per_device, mesh.shape["term"]),
        mesh=mesh,
        in_specs=placed,
        out_specs=(P("topic", "term"), P("topic", "term"), P("term", "topic")),
        check_vma=False,
    )
```

time: 746 us -> 163 us (0.22)
  waiting for transfers between devices: 462 us -> 0 us
  blocking collectives: 225 us -> 0 us
  Pallas kernels: 0 us -> 154 us
  matrix products: 34.3 us -> 0 us
  between operations: 13.8 us -> 0.66 us
    reduce_scatter x3 -> x0, waiting for transfers between devices: 334 us -> none  [the longest x1 278 us: per_device(): lax.psum_scatter(contract_rows(row_block, row_block), 'topic', scatter_di...]
    all_gather x5 -> x0, blocking collectives: 164 us -> none  [the longest x3 94.5 us: apply_gram(): lax.all_gather(current, 'topic', axis=0, tiled=True)]
    pallas_call x0 -> x2, Pallas kernels: none -> 154 us  [the longest x1 149 us: per_device(): pl.pallas_call(functools.partial(codes_kernel, n), out_shape=(jax.ShapeDt...]
    psum x1 -> x0, waiting for transfers between devices: 129 us -> none  [per_device(): gram_rows = lax.psum(gram_part, 'term')]
    all_to_all x1 -> x0, blocking collectives: 60.8 us -> none  [per_device(): lax.all_to_all(factor, 'topic', split_axis=0, concat_axis=1, tiled=True)]
    dot_general x8 -> x0, matrix products: 34.3 us -> none  [the longest x2 14.4 us: contract_rows(): lax.dot_general(left, right, (((0,), (0,)), ((), ())), preferred_element_...]
  transfers between devices with their start and end apart: 4 -> 0, of which waited for: 4 -> 0; matrix products, arithmetic and copies ran while one was open for 2% -> 0% of each run, Pallas kernels for 0% -> 0%
where the time goes in v1:
time: 163 us; the launch traced here: 161 us
  Pallas kernels  154 us (94%)
  local copies, waits for them, and re-layouts  6.6 us (4%)
    pallas_call x1, Pallas kernels, per_device(): pl.pallas_call(functools.partial(codes_kernel, n), out_shape=(jax.ShapeDt...  149 us
    unnamed x14, local copies, waits for them, and re-layouts  6.6 us
    pallas_call x1, Pallas kernels, per_device(): pl.pallas_call(statistic_kernel, grid=(8,), out_shape=jax.ShapeDtypeStruc...  4.85 us

profile of v1, /device:TPU:1, one launch (start us, length us, event | category | flops | bytes accessed | tf_op | source)
XLA Modules:
  0.0 161.0 jit_solution(16324477065664131850)
XLA Ops:
  0.6 0.0 copy-start
  0.6 1.6 copy-done
  2.2 0.0 copy-start.2
  2.2 1.6 copy-done.2
  3.8 0.0 copy-start.3
  3.8 0.8 copy-done.3
  4.7 0.0 copy-start.4
  4.7 0.7 copy-done.4
  5.4 0.0 copy-start.5
  5.4 0.7 copy-done.5
  6.0 0.0 copy-start.1
  6.0 148.9 %codes.1 = (f32[16,128]{1,0:T(8,128)S(1)}, f32[256,128]{1,0:T(8,128)S(1)}, f32[128,128]{1,0:T(8,128)S(1)}) custom-call(bf16[8192,128]{1,0:T(8,128)(2,1)S(1)} %copy-done.2, bf16[8192,128]{1,0:T(8,128)(2,1)S(1)} %copy-done, s32[1,128]{1,0:T(1,128)S(1)} %copy-done.5, f32[16,128]{1,0:T(8,128)S(1)} %bitcast.2, f32[128,128]{1,0:T(8,128)S(1)} %copy-done.3), custom_call_target="tpu_custom_call" | custom-call | tf_op jit(solution)/shard_map/codes/pallas_call | solution.py:402
  155.0 0.0 copy-done.1
  155.0 4.8 %statistic.1 = f32[8192,128]{1,0:T(8,128)} custom-call(bf16[8192,128]{1,0:T(8,128)(2,1)S(1)} %copy-done, s32[1,128]{1,0:T(1,128)S(1)} %copy-done.5, f32[256,128]{1,0:T(8,128)S(1)} %get-tuple-element.8.row, f32[8192,128]{1,0:T(8,128)S(1)} %copy-done.1), custom_call_target="tpu_custom_call" | custom-call | tf_op jit(solution)/shard_map/statistic/pallas_call | solution.py:440
  159.8 0.6 copy.11
  160.4 0.6 copy.12
Async XLA Ops:
  0.6 1.6 copy-start
  2.2 1.6 copy-start.2
  3.8 0.8 copy-start.3
  4.7 0.7 copy-start.4
  5.4 0.7 copy-start.5
  6.0 148.9 %copy-start.1 = (f32[8192,128]{1,0:T(8,128)S(1)}, f32[8192,128]{1,0:T(8,128)}, u32[]{:S(2)}) copy-start(f32[8192,128]{1,0:T(8,128)} %stat.1) | copy-start | bytes 12582916

commit v2 on v1

v2 whole, which is shorter than its diff:
```python
import functools

import jax
import jax.numpy as jnp
from jax import lax
from jax.experimental import pallas as pl
from jax.experimental.pallas import tpu as pltpu
from jax.sharding import PartitionSpec as P

ITERS = 3
EPSILON = 1e-06
DECAY = 0.5
MESH = pl.DeviceIdType.MESH
BF = jnp.bfloat16
F32 = jnp.float32


def split2(value):
    high = value.astype(BF)
    return high, (value - high.astype(F32)).astype(BF)


def dot(left, right):
    return jnp.dot(left, right, preferred_element_type=F32)


def codes_kernel(
    n, factor, tiles, docs_in, codes_in, gram_stat_in,
    codes_out, gram_out, weights_out,
    factor_v, tiles_v, docs, codes, gram_stat,
    xx, xt, own, outgoing, incoming, xin, xsum, zin, zsum, tile,
    gcol, gsend, cbuf, csend, dsend, drecv, fsend, arow, brow,
    local_sem, a2a_send, a2a_recv, core_send, core_recv, y_send, y_recv,
    x_send, x_recv, z_send, z_recv, t_send, t_recv, g_send, g_recv, c_send, c_recv,
    d_send, d_recv, fa_send, fa_recv, fb_send, fb_recv,
):
    rows, topics = factor.shape
    piece = rows // n
    block = codes.shape[0]
    half = n // 2
    sets = half + 1
    ny = n // 4
    nz = n // 2
    slim = topics // n
    d = lax.axis_index("term")
    t = lax.axis_index("topic")
    core = d % 2
    xlo = (d // 2) % 2
    y = d // 4
    xhi = t // nz
    z = t % nz
    sibling = d + 1 - 2 * core

    barrier = pltpu.get_barrier_semaphore()

    def greet(s, carry):
        pl.semaphore_signal(barrier, 1, device_id={"topic": (t + s) % n}, device_id_type=MESH)
        pl.semaphore_signal(barrier, 1, device_id={"term": (d + s) % n}, device_id_type=MESH)
        return carry

    lax.fori_loop(1, n, greet, 0)

    def greet_senders(s, carry):
        @pl.when((s != d) | (t != d))
        def _():
            pl.semaphore_signal(barrier, 1, device_id={"term": s, "topic": d}, device_id_type=MESH)
        return carry

    lax.fori_loop(0, n, greet_senders, 0)
    pl.semaphore_signal(
        barrier, 1,
        device_id={"term": y * 4 + (1 - xlo) * 2 + core, "topic": (1 - xhi) * nz + z},
        device_id_type=MESH,
    )
    loads = [
        pltpu.make_async_copy(a, b, local_sem.at[s])
        for s, (a, b) in enumerate(
            [(factor, factor_v), (tiles, tiles_v), (docs_in, docs), (codes_in, codes),
             (gram_stat_in, gram_stat)]
        )
    ]
    load_own = pltpu.make_async_copy(
        factor.at[pl.ds(t * piece, piece)], xx.at[t, pl.ds(core * piece, piece)], a2a_recv.at[t]
    )
    loads[3].start()
    load_own.start()
    for s in (0, 1, 2, 4):
        loads[s].start()

    @pl.when(t == d)
    def _():
        pl.semaphore_wait(barrier, 3 * n - 2)

    @pl.when(t != d)
    def _():
        pl.semaphore_wait(barrier, 3 * n - 1)

    def send_piece(s, carry):
        p = (t + s) % n
        pltpu.make_async_remote_copy(
            factor.at[pl.ds(p * piece, piece)],
            xx.at[t, pl.ds(core * piece, piece)],
            a2a_send,
            a2a_recv.at[t],
            device_id={"topic": p},
            device_id_type=MESH,
        ).start()
        return carry

    lax.fori_loop(1, n, send_piece, 0)

    def share_codes(step, current):
        high, middle = split2(current)
        csend[step, :block, :] = high
        csend[step, block:, :] = middle

        def send_codes(s, carry):
            pltpu.make_async_remote_copy(
                csend.at[step],
                cbuf.at[step, :, pl.ds(pl.multiple_of(t * topics, topics), topics)],
                c_send.at[step],
                c_recv.at[step],
                device_id={"topic": (t + s) % n},
                device_id_type=MESH,
            ).start()
            return carry

        lax.fori_loop(1, n, send_codes, 0)
        cbuf[step, :, pl.ds(pl.multiple_of(t * topics, topics), topics)] = csend[step]

    loads[3].wait()
    share_codes(0, codes[...])

    for s in (0, 1, 2, 4):
        loads[s].wait()
    share = jnp.zeros((tiles.shape[1], topics), F32)
    for s in range(n):
        part = tiles_v[s * piece:(s + 1) * piece, :]
        share = share + lax.dot_general(
            part, factor_v[s * piece:(s + 1) * piece, :], (((0,), (0,)), ((), ())),
            preferred_element_type=F32,
        )
    picks = (
        lax.broadcasted_iota(jnp.int32, (n * block, tiles.shape[1]), 0) == docs[...]
    ).astype(F32)
    onehot = picks.astype(BF)
    high, middle = split2(share)
    low = (share - high.astype(F32) - middle.astype(F32)).astype(BF)
    spread = dot(onehot, high) + dot(onehot, middle) + dot(onehot, low)
    dsend[...] = spread.reshape(n, block, topics)

    def send_share(s, carry):
        target = (d + s) % n
        pltpu.make_async_remote_copy(
            dsend.at[target], drecv.at[d], d_send, d_recv,
            device_id={"term": target}, device_id_type=MESH,
        ).start()
        return carry

    lax.fori_loop(1, n, send_share, 0)
    drecv[d] = dsend[d]

    def place(p, q):
        k = (p + q) % n
        e1 = (p + n - k // 2 - core) % n
        swap = (e1 + half - 1 + core) // n
        i = p + swap * (q - p)
        j = q + swap * (p - q)
        e = (i + n - k // 2 - core) % n
        return k // 4, (k // 2) % 2, e, i, j

    def pair_count(m):
        return (m - (m + core) % 2 + 2) // 2

    def scale_of(y2):
        return 1.0 + ((y2 * 2 + xlo) * n + t).astype(F32) * (1.0 / (2 * ny * n))

    def forward(p):
        return pltpu.make_async_remote_copy(
            xx.at[p, pl.ds(core * piece, piece)],
            xx.at[p, pl.ds(core * piece, piece)],
            core_send,
            core_recv.at[p],
            device_id={"term": sibling},
            device_id_type=MESH,
        )

    scale = scale_of(y)

    def arrive(m):
        p = (t + n - m) % n
        mine = xx.at[p, pl.ds(core * piece, piece)]
        pltpu.make_async_copy(mine, mine, a2a_recv.at[p]).wait()
        forward(p).start()
        theirs = xx.at[p, pl.ds((1 - core) * piece, piece)]
        pltpu.make_async_copy(theirs, theirs, core_recv.at[p]).wait()
        xt[p] = xx[p].T

        def pair(s, carry):
            q = (t + n - ((m + core) % 2 + 2 * s)) % n
            y2, x2, e, i, j = place(p, q)
            product = dot(xt[i], xx[j])

            @pl.when(y2 == y)
            def _():
                own[x2, e] = product

            @pl.when(y2 != y)
            def _():
                outgoing[y2, x2, e] = (product * scale).astype(BF)
                pltpu.make_async_remote_copy(
                    outgoing.at[y2, x2, e], incoming.at[y, x2, e], y_send, y_recv.at[y, x2, e],
                    device_id={"term": y2 * 4 + xlo * 2 + core}, device_id_type=MESH,
                ).start()

            return carry

        lax.fori_loop(0, pair_count(m), pair, 0)

    def reduce_y(m):
        p = (t + n - m) % n

        def pair(s, carry):
            q = (t + n - ((m + core) % 2 + 2 * s)) % n
            y2, x2, e, i, j = place(p, q)

            @pl.when(y2 == y)
            def _():
                total = own[x2, e]
                for r in range(1, ny):
                    y3 = (y + r) % ny
                    got = incoming.at[y3, x2, e]
                    pltpu.make_async_copy(got, got, y_recv.at[y3, x2, e]).wait()
                    total = total + incoming[y3, x2, e].astype(F32) * (1.0 / scale_of(y3))
                own[x2, e] = total
                for h in range(2):
                    @pl.when((x2 != xlo) | (h != xhi))
                    def _():
                        pltpu.make_async_remote_copy(
                            own.at[x2, e, pl.ds(h * (topics // 2), topics // 2)],
                            xin.at[xlo * 2 + xhi, e],
                            x_send,
                            x_recv.at[xlo * 2 + xhi, e],
                            device_id={"term": y * 4 + x2 * 2 + core, "topic": h * nz + z},
                            device_id_type=MESH,
                        ).start()

            return carry

        lax.fori_loop(0, pair_count(m), pair, 0)

    lag = 2

    def first(m, carry):
        arrive(m)
        return carry

    def both(m, carry):
        arrive(m)
        reduce_y(m - lag)
        return carry

    def last(m, carry):
        reduce_y(m)
        return carry

    lax.fori_loop(0, lag, first, 0)
    lax.fori_loop(lag, n, both, 0)
    lax.fori_loop(n - lag, n, last, 0)

    xsum[sets - 1] = jnp.zeros((topics // 2, topics), F32)

    def reduce_x(e, carry):
        total = own[xlo, e, pl.ds(xhi * (topics // 2), topics // 2), :]
        for r in range(1, 4):
            source = (xlo * 2 + xhi + r) % 4
            got = xin.at[source, e]
            pltpu.make_async_copy(got, got, x_recv.at[source, e]).wait()
            total = total + xin[source, e]
        xsum[e] = total
        return carry

    lax.fori_loop(0, sets - core, reduce_x, 0)

    def send_z(s, carry):
        target = (z + s) % nz
        pltpu.make_async_remote_copy(
            xsum.at[:, pl.ds(target * slim, slim)], zin.at[z], z_send, z_recv,
            device_id={"topic": xhi * nz + target}, device_id_type=MESH,
        ).start()
        return carry

    lax.fori_loop(1, nz, send_z, 0)
    zin[z] = xsum[:, pl.ds(z * slim, slim), :]
    zparts = zin.at[pl.ds(0, nz - 1)]
    pltpu.make_async_copy(zparts, zparts, z_recv).wait()
    total = zin[0]
    for s in range(1, nz):
        total = total + zin[s]
    zsum[...] = total

    def send_slim(s, carry):
        target = (t + s) % n
        e1 = (target + n - d // 2 - core) % n
        swap = (e1 + half - 1 + core) // n
        e = e1 + swap * (n - core - 2 * e1)
        pltpu.make_async_remote_copy(
            zsum.at[e], tile.at[pl.ds(t * slim, slim)], t_send, t_recv,
            device_id={"topic": target}, device_id_type=MESH,
        ).start()
        return carry

    lax.fori_loop(1, n, send_slim, 0)
    role = (t + n - d // 2 - core) % n
    swapped = (role + half - 1 + core) // n
    tile[pl.ds(t * slim, slim), :] = zsum[role + swapped * (n - core - 2 * role)]
    tparts = tile.at[pl.ds(0, topics - slim)]
    pltpu.make_async_copy(tparts, tparts, t_recv).wait()

    @pl.when(swapped == 0)
    def _():
        high, middle = split2(tile[...].T)
        gsend[:, :topics] = high
        gsend[:, topics:] = middle

    @pl.when(swapped != 0)
    def _():
        high, middle = split2(tile[...])
        gsend[:, :topics] = high
        gsend[:, topics:] = middle

    def spot(source):
        return pl.ds(((source + n - t) % n) * topics, topics)

    def send_gram(s, carry):
        pltpu.make_async_remote_copy(
            gsend, gcol.at[spot(d)], g_send, g_recv.at[d],
            device_id={"term": (d + 2 * s) % n}, device_id_type=MESH,
        ).start()
        return carry

    lax.fori_loop(1, half, send_gram, 0)
    pltpu.make_async_remote_copy(
        gsend, gcol.at[spot(d)], g_send, g_recv.at[d],
        device_id={"term": sibling}, device_id_type=MESH,
    ).start()
    gcol[spot(d), :] = gsend[...]

    dparts = drecv.at[pl.ds(0, n - 1)]
    pltpu.make_async_copy(dparts, dparts, d_recv).wait()
    data = drecv[0]
    for s in range(1, n):
        data = data + drecv[s]

    def pass_gram(s, carry):
        source = (d + n - 2 * s) % n
        got = gcol.at[spot(source)]
        pltpu.make_async_copy(got, got, g_recv.at[source]).wait()
        pltpu.make_async_remote_copy(
            got, got, g_send, g_recv.at[source],
            device_id={"term": sibling}, device_id_type=MESH,
        ).start()
        return carry

    lax.fori_loop(1, half, pass_gram, 0)

    def take_gram(s, carry):
        source = (sibling + n - 2 * s) % n
        got = gcol.at[spot(source)]
        pltpu.make_async_copy(got, got, g_recv.at[source]).wait()
        return carry

    lax.fori_loop(0, half, take_gram, 0)

    current = codes[...]
    for step in range(ITERS):
        if step > 0:
            share_codes(step, current)
        cparts = cbuf.at[step, :, pl.ds(0, (n - 1) * topics)]
        pltpu.make_async_copy(cparts, cparts, c_recv.at[step]).wait()
        product = dot(cbuf[step], gcol[...])
        applied = product[:, :topics] + product[:, topics:]
        applied = applied[:block] + applied[block:]
        current = current * data / (applied + EPSILON)

    fsend[...] = current

    def send_row(s, carry):
        pltpu.make_async_remote_copy(
            fsend, arow.at[d], fa_send, fa_recv,
            device_id={"term": (d + s) % n}, device_id_type=MESH,
        ).start()
        return carry

    lax.fori_loop(1, n, send_row, 0)

    def send_column(s, carry):
        target = (t + s) % n

        @pl.when((t != d) | (target != t))
        def _():
            pltpu.make_async_remote_copy(
                fsend, brow.at[d], fb_send, fb_recv,
                device_id={"term": t, "topic": target}, device_id_type=MESH,
            ).start()

        return carry

    lax.fori_loop(0, n, send_column, 0)
    codes_out[...] = current
    arow[d] = current
    choose = picks.T.astype(BF)

    sent = factor.at[pl.ds(0, rows - piece)]
    pltpu.make_async_copy(sent, sent, a2a_send).wait()
    pltpu.make_async_copy(factor, factor, core_send).wait()
    for c in range(2):
        @pl.when(core == c)
        def _():
            if ny > 1:
                y_part = outgoing.at[pl.ds(0, ny - 1), :, pl.ds(0, sets - c)]
                pltpu.make_async_copy(y_part, y_part, y_send).wait()
            x_part = xin.at[pl.ds(0, 3), pl.ds(0, sets - c)]
            pltpu.make_async_copy(x_part, x_part, x_send).wait()

    pltpu.make_async_copy(zparts, zparts, z_send).wait()
    pltpu.make_async_copy(tparts, tparts, t_send).wait()
    gparts = gcol.at[pl.ds(0, (n - 1) * topics)]
    pltpu.make_async_copy(gparts, gparts, g_send).wait()
    pltpu.make_async_copy(dparts, dparts, d_send).wait()
    for step in range(ITERS):
        cparts = cbuf.at[step, :, pl.ds(0, (n - 1) * topics)]
        pltpu.make_async_copy(cparts, cparts, c_send.at[step]).wait()

    aparts = arow.at[pl.ds(0, n - 1)]
    pltpu.make_async_copy(aparts, aparts, fa_recv).wait()
    whole = arow[...].reshape(n * block, topics)
    high, middle = split2(whole)
    weights_out[:, :topics] = dot(choose, high).astype(BF)
    weights_out[:, topics:] = dot(choose, middle).astype(BF)
    a_high, a_middle = split2(whole.T)

    @pl.when(t == d)
    def _():
        brow[d] = current
        bparts = brow.at[pl.ds(0, n - 1)]
        pltpu.make_async_copy(bparts, bparts, fb_recv).wait()
        pltpu.make_async_copy(bparts, bparts, fb_send).wait()

    @pl.when(t != d)
    def _():
        pltpu.make_async_copy(brow, brow, fb_recv).wait()
        pltpu.make_async_copy(brow, brow, fb_send).wait()

    b_high, b_middle = split2(brow[...].reshape(n * block, topics))
    outer = dot(a_high, b_high) + (dot(a_high, b_middle) + dot(a_middle, b_high))
    gram_out[...] = DECAY * gram_stat[...] + outer * (1.0 / (n * block))
    pltpu.make_async_copy(aparts, aparts, fa_send).wait()


def statistic_kernel(scale, tiles, weights, stat, codes, gram, out, codes_out, gram_out):
    topics = stat.shape[1]

    @pl.when(pl.program_id(0) == 0)
    def _():
        codes_out[...] = codes[...]
        gram_out[...] = gram[...]

    product = dot(tiles[...], weights[...])
    product = product[:, :topics] + product[:, topics:]
    out[...] = DECAY * stat[...] + product * scale


def per_device(n, factor, tile_values, tile_docs, codes, gram_stat, data_stat):
    rows, topics = factor.shape
    width = tile_values.shape[1]
    block = codes.shape[1]
    piece = rows // n
    sets = n // 2 + 1
    ny = n // 4
    nz = n // 2
    hbm = pl.BlockSpec(memory_space=pltpu.HBM)
    vmem = pl.BlockSpec(memory_space=pltpu.VMEM)
    dma = pltpu.SemaphoreType.DMA
    codes_t, gram, weights = pl.pallas_call(
        functools.partial(codes_kernel, n),
        out_shape=(
            jax.ShapeDtypeStruct((block, topics), F32),
            jax.ShapeDtypeStruct((topics, topics), F32),
            jax.ShapeDtypeStruct((width, 2 * topics), BF),
        ),
        in_specs=[hbm] * 5,
        out_specs=(vmem, vmem, vmem),
        scratch_shapes=[
            pltpu.VMEM((rows, topics), BF),
            pltpu.VMEM((rows, width), BF),
            pltpu.VMEM((1, width), jnp.int32),
            pltpu.VMEM((block, topics), F32),
            pltpu.VMEM((topics, topics), F32),
            pltpu.VMEM((n, 2 * piece, topics), BF),
            pltpu.VMEM((n, topics, 2 * piece), BF),
            pltpu.VMEM((2, sets, topics, topics), F32),
            pltpu.VMEM((ny, 2, sets, topics, topics), BF),
            pltpu.VMEM((ny, 2, sets, topics, topics), BF),
            pltpu.VMEM((4, sets, topics // 2, topics), F32),
            pltpu.VMEM((sets, topics // 2, topics), F32),
            pltpu.VMEM((nz, sets, topics // n, topics), F32),
            pltpu.VMEM((sets, topics // n, topics), F32),
            pltpu.VMEM((topics, topics), F32),
            pltpu.VMEM((n * topics, 2 * topics), BF),
            pltpu.VMEM((topics, 2 * topics), BF),
            pltpu.VMEM((ITERS, 2 * block, n * topics), BF),
            pltpu.VMEM((ITERS, 2 * block, topics), BF),
            pltpu.VMEM((n, block, topics), F32),
            pltpu.VMEM((n, block, topics), F32),
            pltpu.VMEM((block, topics), F32),
            pltpu.VMEM((n, block, topics), F32),
            pltpu.VMEM((n, block, topics), F32),
            dma((5,)), dma, dma((n,)), dma, dma((n,)), dma, dma((ny, 2, sets)),
            dma, dma((4, sets)), dma, dma, dma, dma, dma, dma((n,)), dma((ITERS,)), dma((ITERS,)),
            dma, dma, dma, dma, dma, dma,
        ],
        compiler_params=pltpu.CompilerParams(
            collective_id=0, has_side_effects=True, vmem_limit_bytes=62 * 1024 * 1024
        ),
        name="codes",
    )(factor, tile_values, tile_docs, codes.T, gram_stat)
    step = rows // 8
    whole = lambda i: (0, 0)
    part = lambda i: (i, 0)
    data_new, codes_new, gram_new = pl.pallas_call(
        functools.partial(statistic_kernel, 1.0 / (n * block)),
        grid=(8,),
        out_shape=(
            jax.ShapeDtypeStruct((rows, topics), F32),
            jax.ShapeDtypeStruct((block, topics), F32),
            jax.ShapeDtypeStruct((topics, topics), F32),
        ),
        in_specs=[
            pl.BlockSpec((step, width), part),
            pl.BlockSpec((width, 2 * topics), whole),
            pl.BlockSpec((step, topics), part),
            pl.BlockSpec((block, topics), whole),
            pl.BlockSpec((topics, topics), whole),
        ],
        out_specs=(
            pl.BlockSpec((step, topics), part),
            pl.BlockSpec((block, topics), whole),
            pl.BlockSpec((topics, topics), whole),
        ),
        compiler_params=pltpu.CompilerParams(vmem_limit_bytes=62 * 1024 * 1024),
        name="statistic",
    )(tile_values, weights, data_stat, codes_t, gram)
    return codes_new.T, gram_new, data_new


def solution(mesh):
    placed = (
        P("term", "topic"),
        P("term", None),
        P("term", None),
        P("topic", "term"),
        P("topic", "term"),
        P("term", "topic"),
    )
    return jax.shard_map(
        functools.partial(per_device, mesh.shape["term"]),
        mesh=mesh,
        in_specs=placed,
        out_specs=(P("topic", "term"), P("topic", "term"), P("term", "topic")),
        check_vma=False,
    )
```

time: 163 us -> 146 us (0.90)
  Pallas kernels: 154 us -> 145 us
  local copies, waits for them, and re-layouts: 6.6 us -> 0 us
    pallas_call x1, Pallas kernels: 149 us -> 137 us  [per_device(): pl.pallas_call(functools.partial(codes_kernel, n), out_shape=(jax.ShapeDt...]
    unnamed x14 -> x0, local copies, waits for them, and re-layouts: 6.6 us -> none
    pallas_call x1, Pallas kernels: 4.85 us -> 7.94 us  [per_device(): pl.pallas_call(functools.partial(statistic_kernel, 1.0 / (n * block)), gr...]
where the time goes in v2:
time: 146 us
  Pallas kernels  145 us (99%)
    pallas_call x1, Pallas kernels, per_device(): pl.pallas_call(functools.partial(codes_kernel, n), out_shape=(jax.ShapeDt...  137 us
    pallas_call x1, Pallas kernels, per_device(): pl.pallas_call(functools.partial(statistic_kernel, 1.0 / (n * block)), gr...  7.94 us

profile of v2, /device:TPU:1, one launch (start us, length us, event | category | flops | bytes accessed | tf_op | source)
XLA Modules:
  0.0 145.6 jit_solution(5566691455678082923)
XLA Ops:
  0.6 137.0 %codes.1 = (f32[16,128]{1,0:T(8,128)}, f32[128,128]{1,0:T(8,128)}, bf16[128,256]{1,0:T(8,128)(2,1)}) custom-call(bf16[8192,128]{1,0:T(8,128)(2,1)} %factor.1, bf16[8192,128]{1,0:T(8,128)(2,1)} %tiles.3, s32[1,128]{1,0:T(1,128)} %docs_in.1, f32[16,128]{1,0:T(8,128)} %bitcast.2, f32[128,128]{1,0:T(8,128)} %gram_stat_in.1), custom_call_target="tpu_custom_call" | custom-call | tf_op jit(solution)/shard_map/codes/pallas_call | solution.py:485
  137.7 7.9 %statistic.1 = (f32[8192,128]{1,0:T(8,128)}, f32[16,128]{1,0:T(8,128)}, f32[128,128]{1,0:T(8,128)}) custom-call(bf16[8192,128]{1,0:T(8,128)(2,1)} %tiles.3, bf16[128,256]{1,0:T(8,128)(2,1)} %get-tuple-element.9.weights, f32[8192,128]{1,0:T(8,128)} %stat.1, f32[16,128]{1,0:T(8,128)} %get-tuple-element.10.codes, f32[128,128]{1,0:T(8,128)} %get-tuple-element.11.gram), custom_call_target="tpu_custom_call" | custom-call | tf_op jit(solution)/shard_map/statistic/pallas_call | solution.py:531

commit v3 on v2

--- a/solution.py
+++ b/solution.py
@@ -10,6 +10,9 @@
 ITERS = 3
 EPSILON = 1e-06
 DECAY = 0.5
+LAG_Y = 2
+LAG_X = 4
+HOLD = 11
 MESH = pl.DeviceIdType.MESH
 BF = jnp.bfloat16
 F32 = jnp.float32
@@ -18,6 +21,14 @@
 def split2(value):
     high = value.astype(BF)
     return high, (value - high.astype(F32)).astype(BF)
+
+
+def rem(value, count):
+    return lax.rem(value, jnp.int32(count))
+
+
+def quo(value, count):
+    return lax.div(value, jnp.int32(count))
 
 
 def dot(left, right):
@@ -28,34 +39,36 @@
     n, factor, tiles, docs_in, codes_in, gram_stat_in,
     codes_out, gram_out, weights_out,
     factor_v, tiles_v, docs, codes, gram_stat,
-    xx, xt, own, outgoing, incoming, xin, xsum, zin, zsum, tile,
+    xx, xt, product, own, outgoing, incoming, xin, xsum, zin, zsum, tile,
     gcol, gsend, cbuf, csend, dsend, drecv, fsend, arow, brow,
     local_sem, a2a_send, a2a_recv, core_send, core_recv, y_send, y_recv,
     x_send, x_recv, z_send, z_recv, t_send, t_recv, g_send, g_recv, c_send, c_recv,
     d_send, d_recv, fa_send, fa_recv, fb_send, fb_recv,
 ):
     rows, topics = factor.shape
+    width = tiles.shape[1]
     piece = rows // n
     block = codes.shape[0]
     half = n // 2
     sets = half + 1
+    group = min(4, half)
     ny = n // 4
     nz = n // 2
     slim = topics // n
     d = lax.axis_index("term")
     t = lax.axis_index("topic")
-    core = d % 2
-    xlo = (d // 2) % 2
-    y = d // 4
-    xhi = t // nz
-    z = t % nz
+    core = rem(d, 2)
+    xlo = rem(quo(d, 2), 2)
+    y = quo(d, 4)
+    xhi = quo(t, nz)
+    z = rem(t, nz)
     sibling = d + 1 - 2 * core
 
     barrier = pltpu.get_barrier_semaphore()
 
     def greet(s, carry):
-        pl.semaphore_signal(barrier, 1, device_id={"topic": (t + s) % n}, device_id_type=MESH)
-        pl.semaphore_signal(barrier, 1, device_id={"term": (d + s) % n}, device_id_type=MESH)
+        pl.semaphore_signal(barrier, 1, device_id={"topic": rem(t + s, n)}, device_id_type=MESH)
+        pl.semaphore_signal(barrier, 1, device_id={"term": rem(d + s, n)}, device_id_type=MESH)
         return carry
 
     lax.fori_loop(1, n, greet, 0)
@@ -95,19 +108,29 @@
     def _():
         pl.semaphore_wait(barrier, 3 * n - 1)
 
+    def piece_at(m):
+        u = quo(m, 2)
+        odd = rem(u, 2)
+        offset = odd * quo(u + 1, 2) + (1 - odd) * (nz - quo(u, 2))
+        return rem(m, 2) * nz + rem(z + offset, nz)
+
     def send_piece(s, carry):
-        p = (t + s) % n
-        pltpu.make_async_remote_copy(
-            factor.at[pl.ds(p * piece, piece)],
-            xx.at[t, pl.ds(core * piece, piece)],
-            a2a_send,
-            a2a_recv.at[t],
-            device_id={"topic": p},
-            device_id_type=MESH,
-        ).start()
-        return carry
-
-    lax.fori_loop(1, n, send_piece, 0)
+        p = piece_at(s)
+
+        @pl.when(p != t)
+        def _():
+            pltpu.make_async_remote_copy(
+                factor.at[pl.ds(p * piece, piece)],
+                xx.at[t, pl.ds(core * piece, piece)],
+                a2a_send,
+                a2a_recv.at[t],
+                device_id={"topic": p},
+                device_id_type=MESH,
+            ).start()
+
+        return carry
+
+    lax.fori_loop(0, n - 2, send_piece, 0)
 
     def share_codes(step, current):
         high, middle = split2(current)
@@ -120,7 +143,7 @@
                 cbuf.at[step, :, pl.ds(pl.multiple_of(t * topics, topics), topics)],
                 c_send.at[step],
                 c_recv.at[step],
-                device_id={"topic": (t + s) % n},
+                device_id={"topic": rem(t + s, n)},
                 device_id_type=MESH,
             ).start()
             return carry
@@ -128,11 +151,9 @@
         lax.fori_loop(1, n, send_codes, 0)
         cbuf[step, :, pl.ds(pl.multiple_of(t * topics, topics), topics)] = csend[step]
 
-    loads[3].wait()
-    share_codes(0, codes[...])
-
-    for s in (0, 1, 2, 4):
-        loads[s].wait()
+
+    for load in loads:
+        load.wait()
     share = jnp.zeros((tiles.shape[1], topics), F32)
     for s in range(n):
         part = tiles_v[s * piece:(s + 1) * piece, :]
@@ -150,7 +171,7 @@
     dsend[...] = spread.reshape(n, block, topics)
 
     def send_share(s, carry):
-        target = (d + s) % n
+        target = rem(d + s, n)
         pltpu.make_async_remote_copy(
             dsend.at[target], drecv.at[d], d_send, d_recv,
             device_id={"term": target}, device_id_type=MESH,
@@ -161,53 +182,71 @@
     drecv[d] = dsend[d]
 
     def place(p, q):
-        k = (p + q) % n
-        e1 = (p + n - k // 2 - core) % n
-        swap = (e1 + half - 1 + core) // n
-        i = p + swap * (q - p)
-        j = q + swap * (p - q)
-        e = (i + n - k // 2 - core) % n
-        return k // 4, (k // 2) % 2, e, i, j
+        k = rem(p + q, n)
+        k_half = quo(k, 2)
+        e1 = rem(p + n - k_half - core, n)
+        swap = quo(e1 + half - 1 + core, n)
+        e = e1 + swap * (n - core - 2 * e1)
+        return quo(k_half, 2), rem(k_half, 2), e, swap
+
+    def side_of(m):
+        return rem(quo(quo(m, 2) + 1, 2), 2)
 
     def pair_count(m):
-        return (m - (m + core) % 2 + 2) // 2
+        u = quo(m, 2)
+        return core * 2 * quo(u + 1, 2) + (1 - core) * (2 * quo(u, 2) + rem(m, 2) + 1)
+
+    def partner(side, s):
+        rank = quo(s, 2)
+        return piece_at(4 * rank + 2 * rem(rank + side, 2) + rem(s, 2))
 
     def scale_of(y2):
         return 1.0 + ((y2 * 2 + xlo) * n + t).astype(F32) * (1.0 / (2 * ny * n))
 
-    def forward(p):
-        return pltpu.make_async_remote_copy(
-            xx.at[p, pl.ds(core * piece, piece)],
-            xx.at[p, pl.ds(core * piece, piece)],
-            core_send,
-            core_recv.at[p],
-            device_id={"term": sibling},
-            device_id_type=MESH,
-        )
-
     scale = scale_of(y)
+    unscale = [1.0 / scale_of(rem(y + r, ny)) for r in range(ny)]
+    xsum[sets - 1] = jnp.zeros((topics // 2, topics), F32)
 
     def arrive(m):
-        p = (t + n - m) % n
+        p = piece_at(m)
         mine = xx.at[p, pl.ds(core * piece, piece)]
+        theirs = xx.at[p, pl.ds((1 - core) * piece, piece)]
         pltpu.make_async_copy(mine, mine, a2a_recv.at[p]).wait()
-        forward(p).start()
-        theirs = xx.at[p, pl.ds((1 - core) * piece, piece)]
+        pltpu.make_async_remote_copy(
+            mine, mine, core_send, core_recv.at[p],
+            device_id={"term": sibling}, device_id_type=MESH,
+        ).start()
+
+        @pl.when(m == min(HOLD, n - 3))
+        def _():
+            lax.fori_loop(n - 2, n, send_piece, 0)
+
         pltpu.make_async_copy(theirs, theirs, core_recv.at[p]).wait()
-        xt[p] = xx[p].T
+        xt[side_of(m), 2 * quo(m, 4) + rem(m, 2)] = xx[p].T
+        side = rem(side_of(m) + core, 2)
+        count = pair_count(m)
+
+        def multiply(g, carry):
+            left = xt[side, pl.ds(g * group, group)].reshape(group * topics, 2 * piece)
+            product[pl.ds(g * group, group)] = dot(left, xx[p]).reshape(group, topics, topics)
+            return carry
+
+        lax.fori_loop(0, quo(count + group - 1, group), multiply, 0)
 
         def pair(s, carry):
-            q = (t + n - ((m + core) % 2 + 2 * s)) % n
-            y2, x2, e, i, j = place(p, q)
-            product = dot(xt[i], xx[j])
+            y2, x2, e, swap = place(p, partner(side, s))
+
+            @pl.when(swap == 0)
+            def _():
+                product[s] = product[s].T
 
             @pl.when(y2 == y)
             def _():
-                own[x2, e] = product
+                own[x2, e] = product[s]
 
             @pl.when(y2 != y)
             def _():
-                outgoing[y2, x2, e] = (product * scale).astype(BF)
+                outgoing[y2, x2, e] = (product[s] * scale).astype(BF)
                 pltpu.make_async_remote_copy(
                     outgoing.at[y2, x2, e], incoming.at[y, x2, e], y_send, y_recv.at[y, x2, e],
                     device_id={"term": y2 * 4 + xlo * 2 + core}, device_id_type=MESH,
@@ -215,82 +254,92 @@
 
             return carry
 
+        lax.fori_loop(0, count, pair, 0)
+
+    def walk(m, body):
+        p = piece_at(m)
+        side = rem(side_of(m) + core, 2)
+
+        def pair(s, carry):
+            y2, x2, e, swap = place(p, partner(side, s))
+            body(y2, x2, e)
+            return carry
+
         lax.fori_loop(0, pair_count(m), pair, 0)
 
-    def reduce_y(m):
-        p = (t + n - m) % n
-
-        def pair(s, carry):
-            q = (t + n - ((m + core) % 2 + 2 * s)) % n
-            y2, x2, e, i, j = place(p, q)
-
-            @pl.when(y2 == y)
-            def _():
-                total = own[x2, e]
-                for r in range(1, ny):
-                    y3 = (y + r) % ny
-                    got = incoming.at[y3, x2, e]
-                    pltpu.make_async_copy(got, got, y_recv.at[y3, x2, e]).wait()
-                    total = total + incoming[y3, x2, e].astype(F32) * (1.0 / scale_of(y3))
-                own[x2, e] = total
-                for h in range(2):
-                    @pl.when((x2 != xlo) | (h != xhi))
-                    def _():
-                        pltpu.make_async_remote_copy(
-                            own.at[x2, e, pl.ds(h * (topics // 2), topics // 2)],
-                            xin.at[xlo * 2 + xhi, e],
-                            x_send,
-                            x_recv.at[xlo * 2 + xhi, e],
-                            device_id={"term": y * 4 + x2 * 2 + core, "topic": h * nz + z},
-                            device_id_type=MESH,
-                        ).start()
-
+    def reduce_y(y2, x2, e):
+        @pl.when(y2 == y)
+        def _():
+            total = own[x2, e]
+            for r in range(1, ny):
+                y3 = rem(y + r, ny)
+                got = incoming.at[y3, x2, e]
+                pltpu.make_async_copy(got, got, y_recv.at[y3, x2, e]).wait()
+                total = total + incoming[y3, x2, e].astype(F32) * unscale[r]
+            own[x2, e] = total
+            for h in range(2):
+                @pl.when((x2 != xlo) | (h != xhi))
+                def _():
+                    pltpu.make_async_remote_copy(
+                        own.at[x2, e, pl.ds(h * (topics // 2), topics // 2)],
+                        xin.at[xlo * 2 + xhi, e],
+                        x_send,
+                        x_recv.at[xlo * 2 + xhi, e],
+                        device_id={"term": y * 4 + x2 * 2 + core, "topic": h * nz + z},
+                        device_id_type=MESH,
+                    ).start()
+
+    def reduce_x(y2, x2, e):
+        @pl.when((y2 == y) & (x2 == xlo))
+        def _():
+            total = own[xlo, e, pl.ds(xhi * (topics // 2), topics // 2), :]
+            for r in range(1, 4):
+                source = rem(xlo * 2 + xhi + r, 4)
+                got = xin.at[source, e]
+                pltpu.make_async_copy(got, got, x_recv.at[source, e]).wait()
+                total = total + xin[source, e]
+            xsum[e] = total
+            send_z(e)
+
+    def send_z(e):
+        def send(s, carry):
+            target = rem(z + s, nz)
+            pltpu.make_async_remote_copy(
+                xsum.at[e, pl.ds(target * slim, slim)], zin.at[z, e], z_send, z_recv,
+                device_id={"topic": xhi * nz + target}, device_id_type=MESH,
+            ).start()
             return carry
 
-        lax.fori_loop(0, pair_count(m), pair, 0)
-
-    lag = 2
-
-    def first(m, carry):
-        arrive(m)
-        return carry
-
-    def both(m, carry):
-        arrive(m)
-        reduce_y(m - lag)
-        return carry
-
-    def last(m, carry):
-        reduce_y(m)
-        return carry
-
-    lax.fori_loop(0, lag, first, 0)
-    lax.fori_loop(lag, n, both, 0)
-    lax.fori_loop(n - lag, n, last, 0)
-
-    xsum[sets - 1] = jnp.zeros((topics // 2, topics), F32)
-
-    def reduce_x(e, carry):
-        total = own[xlo, e, pl.ds(xhi * (topics // 2), topics // 2), :]
-        for r in range(1, 4):
-            source = (xlo * 2 + xhi + r) % 4
-            got = xin.at[source, e]
-            pltpu.make_async_copy(got, got, x_recv.at[source, e]).wait()
-            total = total + xin[source, e]
-        xsum[e] = total
-        return carry
-
-    lax.fori_loop(0, sets - core, reduce_x, 0)
-
-    def send_z(s, carry):
-        target = (z + s) % nz
-        pltpu.make_async_remote_copy(
-            xsum.at[:, pl.ds(target * slim, slim)], zin.at[z], z_send, z_recv,
-            device_id={"topic": xhi * nz + target}, device_id_type=MESH,
-        ).start()
-        return carry
-
-    lax.fori_loop(1, nz, send_z, 0)
+        lax.fori_loop(1, nz, send, 0)
+
+    @pl.when(core == 1)
+    def _():
+        send_z(sets - 1)
+
+    def steps(start, stop, first_lag, second_lag):
+        def step(m, carry):
+            if first_lag >= 0:
+                arrive(m)
+            if second_lag >= 1:
+                walk(m - LAG_Y, reduce_y)
+            if second_lag >= 2:
+                walk(m - LAG_X, reduce_x)
+            return carry
+
+        lax.fori_loop(start, stop, step, 0)
+
+    steps(0, LAG_Y, 0, 0)
+    steps(LAG_Y, min(LAG_X, n), 0, 1)
+    steps(LAG_X, n, 0, 2)
+    share_codes(0, codes[...])
+    steps(n, n + LAG_Y, -1, 2)
+
+    def drain(m, carry):
+        walk(m, reduce_x)
+        return carry
+
+    lax.fori_loop(n + LAG_Y - LAG_X, n, drain, 0)
+
     zin[z] = xsum[:, pl.ds(z * slim, slim), :]
     zparts = zin.at[pl.ds(0, nz - 1)]
     pltpu.make_async_copy(zparts, zparts, z_recv).wait()
@@ -300,9 +349,9 @@
     zsum[...] = total
 
     def send_slim(s, carry):
-        target = (t + s) % n
-        e1 = (target + n - d // 2 - core) % n
-        swap = (e1 + half - 1 + core) // n
+        target = rem(t + s, n)
+        e1 = rem(target + n - quo(d, 2) - core, n)
+        swap = quo(e1 + half - 1 + core, n)
         e = e1 + swap * (n - core - 2 * e1)
         pltpu.make_async_remote_copy(
             zsum.at[e], tile.at[pl.ds(t * slim, slim)], t_send, t_recv,
@@ -311,8 +360,8 @@
         return carry
 
     lax.fori_loop(1, n, send_slim, 0)
-    role = (t + n - d // 2 - core) % n
-    swapped = (role + half - 1 + core) // n
+    role = rem(t + n - quo(d, 2) - core, n)
+    swapped = quo(role + half - 1 + core, n)
     tile[pl.ds(t * slim, slim), :] = zsum[role + swapped * (n - core - 2 * role)]
     tparts = tile.at[pl.ds(0, topics - slim)]
     pltpu.make_async_copy(tparts, tparts, t_recv).wait()
@@ -330,12 +379,12 @@
         gsend[:, topics:] = middle
 
     def spot(source):
-        return pl.ds(((source + n - t) % n) * topics, topics)
+        return pl.ds(rem(source + n - t, n) * topics, topics)
 
     def send_gram(s, carry):
         pltpu.make_async_remote_copy(
             gsend, gcol.at[spot(d)], g_send, g_recv.at[d],
-            device_id={"term": (d + 2 * s) % n}, device_id_type=MESH,
+            device_id={"term": rem(d + 2 * s, n)}, device_id_type=MESH,
         ).start()
         return carry
 
@@ -353,7 +402,7 @@
         data = data + drecv[s]
 
     def pass_gram(s, carry):
-        source = (d + n - 2 * s) % n
+        source = rem(d + n - 2 * s, n)
         got = gcol.at[spot(source)]
         pltpu.make_async_copy(got, got, g_recv.at[source]).wait()
         pltpu.make_async_remote_copy(
@@ -365,7 +414,7 @@
     lax.fori_loop(1, half, pass_gram, 0)
 
     def take_gram(s, carry):
-        source = (sibling + n - 2 * s) % n
+        source = rem(sibling + n - 2 * s, n)
         got = gcol.at[spot(source)]
         pltpu.make_async_copy(got, got, g_recv.at[source]).wait()
         return carry
@@ -378,8 +427,8 @@
             share_codes(step, current)
         cparts = cbuf.at[step, :, pl.ds(0, (n - 1) * topics)]
         pltpu.make_async_copy(cparts, cparts, c_recv.at[step]).wait()
-        product = dot(cbuf[step], gcol[...])
-        applied = product[:, :topics] + product[:, topics:]
+        applied = dot(cbuf[step], gcol[...])
+        applied = applied[:, :topics] + applied[:, topics:]
         applied = applied[:block] + applied[block:]
         current = current * data / (applied + EPSILON)
 
@@ -388,14 +437,14 @@
     def send_row(s, carry):
         pltpu.make_async_remote_copy(
             fsend, arow.at[d], fa_send, fa_recv,
-            device_id={"term": (d + s) % n}, device_id_type=MESH,
+            device_id={"term": rem(d + s, n)}, device_id_type=MESH,
         ).start()
         return carry
 
     lax.fori_loop(1, n, send_row, 0)
 
     def send_column(s, carry):
-        target = (t + s) % n
+        target = rem(t + s, n)
 
         @pl.when((t != d) | (target != t))
         def _():
@@ -436,8 +485,9 @@
     pltpu.make_async_copy(aparts, aparts, fa_recv).wait()
     whole = arow[...].reshape(n * block, topics)
     high, middle = split2(whole)
-    weights_out[:, :topics] = dot(choose, high).astype(BF)
-    weights_out[:, topics:] = dot(choose, middle).astype(BF)
+    share_of_one = 1.0 / (n * block)
+    weights_out[:width, :] = (dot(choose, high) * share_of_one).astype(BF)
+    weights_out[width:, :] = (dot(choose, middle) * share_of_one).astype(BF)
     a_high, a_middle = split2(whole.T)
 
     @pl.when(t == d)
@@ -458,17 +508,14 @@
     pltpu.make_async_copy(aparts, aparts, fa_send).wait()
 
 
-def statistic_kernel(scale, tiles, weights, stat, codes, gram, out, codes_out, gram_out):
-    topics = stat.shape[1]
-
+def statistic_kernel(tiles, weights, stat, codes, gram, out, codes_out, gram_out):
     @pl.when(pl.program_id(0) == 0)
     def _():
         codes_out[...] = codes[...]
         gram_out[...] = gram[...]
 
-    product = dot(tiles[...], weights[...])
-    product = product[:, :topics] + product[:, topics:]
-    out[...] = DECAY * stat[...] + product * scale
+    part = tiles[...]
+    out[...] = DECAY * stat[...] + dot(jnp.concatenate([part, part], axis=1), weights[...])
 
 
 def per_device(n, factor, tile_values, tile_docs, codes, gram_stat, data_stat):
@@ -487,7 +534,7 @@
         out_shape=(
             jax.ShapeDtypeStruct((block, topics), F32),
             jax.ShapeDtypeStruct((topics, topics), F32),
-            jax.ShapeDtypeStruct((width, 2 * topics), BF),
+            jax.ShapeDtypeStruct((2 * width, topics), BF),
         ),
         in_specs=[hbm] * 5,
         out_specs=(vmem, vmem, vmem),
@@ -498,7 +545,8 @@
             pltpu.VMEM((block, topics), F32),
             pltpu.VMEM((topics, topics), F32),
             pltpu.VMEM((n, 2 * piece, topics), BF),
-            pltpu.VMEM((n, topics, 2 * piece), BF),
+            pltpu.VMEM((2, n // 2, topics, 2 * piece), BF),
+            pltpu.VMEM((n // 2, topics, topics), F32),
             pltpu.VMEM((2, sets, topics, topics), F32),
             pltpu.VMEM((ny, 2, sets, topics, topics), BF),
             pltpu.VMEM((ny, 2, sets, topics, topics), BF),
@@ -529,7 +577,7 @@
     whole = lambda i: (0, 0)
     part = lambda i: (i, 0)
     data_new, codes_new, gram_new = pl.pallas_call(
-        functools.partial(statistic_kernel, 1.0 / (n * block)),
+        statistic_kernel,
         grid=(8,),
         out_shape=(
             jax.ShapeDtypeStruct((rows, topics), F32),
@@ -538,7 +586,7 @@
         ),
         in_specs=[
             pl.BlockSpec((step, width), part),
-            pl.BlockSpec((width, 2 * topics), whole),
+            pl.BlockSpec((2 * width, topics), whole),
             pl.BlockSpec((step, topics), part),
             pl.BlockSpec((block, topics), whole),
             pl.BlockSpec((topics, topics), whole),

time: 146 us -> 137 us (0.938)
  Pallas kernels: 145 us -> 135 us
    pallas_call x1, Pallas kernels: 137 us -> 127 us  [per_device(): pl.pallas_call(functools.partial(codes_kernel, n), out_shape=(jax.ShapeDt...]
where the time goes in v3:
time: 137 us; the launch traced here: 135 us
  Pallas kernels  135 us (99%)
    pallas_call x1, Pallas kernels, per_device(): pl.pallas_call(functools.partial(codes_kernel, n), out_shape=(jax.ShapeDt...  127 us
    pallas_call x1, Pallas kernels, per_device(): pl.pallas_call(statistic_kernel, grid=(8,), out_shape=(jax.ShapeDtypeStru...  7.98 us

profile of v3, /device:TPU:1, one launch (start us, length us, event | category | flops | bytes accessed | tf_op | source)
XLA Modules:
  0.0 135.5 jit_solution(2013754291910152589)
XLA Ops:
  0.6 126.9 %codes.1 = (f32[16,128]{1,0:T(8,128)}, f32[128,128]{1,0:T(8,128)}, bf16[256,128]{1,0:T(8,128)(2,1)}) custom-call(bf16[8192,128]{1,0:T(8,128)(2,1)} %factor.1, bf16[8192,128]{1,0:T(8,128)(2,1)} %tiles.3, s32[1,128]{1,0:T(1,128)} %docs_in.1, f32[16,128]{1,0:T(8,128)} %bitcast.2, f32[128,128]{1,0:T(8,128)} %gram_stat_in.1), custom_call_target="tpu_custom_call" | custom-call | tf_op jit(solution)/shard_map/codes/pallas_call | solution.py:532
  127.5 8.0 %statistic.1 = (f32[8192,128]{1,0:T(8,128)}, f32[16,128]{1,0:T(8,128)}, f32[128,128]{1,0:T(8,128)}) custom-call(bf16[8192,128]{1,0:T(8,128)(2,1)} %tiles.3, bf16[256,128]{1,0:T(8,128)(2,1)} %get-tuple-element.9.weights, f32[8192,128]{1,0:T(8,128)} %stat.1, f32[16,128]{1,0:T(8,128)} %get-tuple-element.10.codes, f32[128,128]{1,0:T(8,128)} %get-tuple-element.11.gram), custom_call_target="tpu_custom_call" | custom-call | tf_op jit(solution)/shard_map/statistic/pallas_call | solution.py:579

commit v4 on v3

--- a/solution.py
+++ b/solution.py
@@ -10,9 +10,10 @@
 ITERS = 3
 EPSILON = 1e-06
 DECAY = 0.5
-LAG_Y = 2
-LAG_X = 4
-HOLD = 11
+PARTS = 4
+LAG_Y = 3
+LAG_X = 6
+HOLD = 10
 MESH = pl.DeviceIdType.MESH
 BF = jnp.bfloat16
 F32 = jnp.float32
@@ -138,17 +139,22 @@
         csend[step, block:, :] = middle
 
         def send_codes(s, carry):
-            pltpu.make_async_remote_copy(
-                csend.at[step],
-                cbuf.at[step, :, pl.ds(pl.multiple_of(t * topics, topics), topics)],
-                c_send.at[step],
-                c_recv.at[step],
-                device_id={"topic": rem(t + s, n)},
-                device_id_type=MESH,
-            ).start()
+            target = piece_at(n - 1 - s)
+
+            @pl.when(target != t)
+            def _():
+                pltpu.make_async_remote_copy(
+                    csend.at[step],
+                    cbuf.at[step, :, pl.ds(pl.multiple_of(t * topics, topics), topics)],
+                    c_send.at[step],
+                    c_recv.at[step],
+                    device_id={"topic": target},
+                    device_id_type=MESH,
+                ).start()
+
             return carry
 
-        lax.fori_loop(1, n, send_codes, 0)
+        lax.fori_loop(0, n, send_codes, 0)
         cbuf[step, :, pl.ds(pl.multiple_of(t * topics, topics), topics)] = csend[step]
 
 
@@ -349,17 +355,21 @@
     zsum[...] = total
 
     def send_slim(s, carry):
-        target = rem(t + s, n)
+        target = piece_at(n - 1 - s)
         e1 = rem(target + n - quo(d, 2) - core, n)
         swap = quo(e1 + half - 1 + core, n)
         e = e1 + swap * (n - core - 2 * e1)
-        pltpu.make_async_remote_copy(
-            zsum.at[e], tile.at[pl.ds(t * slim, slim)], t_send, t_recv,
-            device_id={"topic": target}, device_id_type=MESH,
-        ).start()
-        return carry
-
-    lax.fori_loop(1, n, send_slim, 0)
+
+        @pl.when(target != t)
+        def _():
+            pltpu.make_async_remote_copy(
+                zsum.at[e], tile.at[pl.ds(t * slim, slim)], t_send, t_recv,
+                device_id={"topic": target}, device_id_type=MESH,
+            ).start()
+
+        return carry
+
+    lax.fori_loop(0, n, send_slim, 0)
     role = rem(t + n - quo(d, 2) - core, n)
     swapped = quo(role + half - 1 + core, n)
     tile[pl.ds(t * slim, slim), :] = zsum[role + swapped * (n - core - 2 * role)]
@@ -434,6 +444,19 @@
 
     fsend[...] = current
 
+    def send_column(s, carry):
+        target = piece_at(n - 1 - s)
+
+        @pl.when((t != d) | (target != t))
+        def _():
+            pltpu.make_async_remote_copy(
+                fsend, brow.at[d], fb_send, fb_recv,
+                device_id={"term": t, "topic": target}, device_id_type=MESH,
+            ).start()
+
+        return carry
+
+    lax.fori_loop(0, n, send_column, 0)
     def send_row(s, carry):
         pltpu.make_async_remote_copy(
             fsend, arow.at[d], fa_send, fa_recv,
@@ -443,19 +466,6 @@
 
     lax.fori_loop(1, n, send_row, 0)
 
-    def send_column(s, carry):
-        target = rem(t + s, n)
-
-        @pl.when((t != d) | (target != t))
-        def _():
-            pltpu.make_async_remote_copy(
-                fsend, brow.at[d], fb_send, fb_recv,
-                device_id={"term": t, "topic": target}, device_id_type=MESH,
-            ).start()
-
-        return carry
-
-    lax.fori_loop(0, n, send_column, 0)
     codes_out[...] = current
     arow[d] = current
     choose = picks.T.astype(BF)
@@ -508,14 +518,39 @@
     pltpu.make_async_copy(aparts, aparts, fa_send).wait()
 
 
-def statistic_kernel(tiles, weights, stat, codes, gram, out, codes_out, gram_out):
-    @pl.when(pl.program_id(0) == 0)
-    def _():
-        codes_out[...] = codes[...]
-        gram_out[...] = gram[...]
-
-    part = tiles[...]
-    out[...] = DECAY * stat[...] + dot(jnp.concatenate([part, part], axis=1), weights[...])
+def statistic_kernel(
+    parts, tiles, weights, stat, codes, gram, out, codes_out, gram_out,
+    tiles_v, stat_v, out_v, tile_sem, stat_sem, out_sem,
+):
+    rows = tiles.shape[0] // parts
+
+    def load(s):
+        where = pl.ds(s * rows, rows)
+        return (
+            pltpu.make_async_copy(tiles.at[where], tiles_v.at[where], tile_sem.at[s]),
+            pltpu.make_async_copy(stat.at[where], stat_v.at[where], stat_sem.at[s]),
+        )
+
+    def store(s):
+        where = pl.ds(s * rows, rows)
+        return pltpu.make_async_copy(out_v.at[where], out.at[where], out_sem.at[s])
+
+    for s in range(parts):
+        for copy in load(s):
+            copy.start()
+    codes_out[...] = codes[...]
+    gram_out[...] = gram[...]
+    for s in range(parts):
+        for copy in load(s):
+            copy.wait()
+        where = pl.ds(s * rows, rows)
+        part = tiles_v[where, :]
+        out_v[where, :] = DECAY * stat_v[where, :] + dot(
+            jnp.concatenate([part, part], axis=1), weights[...]
+        )
+        store(s).start()
+    for s in range(parts):
+        store(s).wait()
 
 
 def per_device(n, factor, tile_values, tile_docs, codes, gram_stat, data_stat):
@@ -573,29 +608,22 @@
         ),
         name="codes",
     )(factor, tile_values, tile_docs, codes.T, gram_stat)
-    step = rows // 8
-    whole = lambda i: (0, 0)
-    part = lambda i: (i, 0)
+    parts = PARTS
     data_new, codes_new, gram_new = pl.pallas_call(
-        statistic_kernel,
-        grid=(8,),
+        functools.partial(statistic_kernel, parts),
         out_shape=(
             jax.ShapeDtypeStruct((rows, topics), F32),
             jax.ShapeDtypeStruct((block, topics), F32),
             jax.ShapeDtypeStruct((topics, topics), F32),
         ),
-        in_specs=[
-            pl.BlockSpec((step, width), part),
-            pl.BlockSpec((2 * width, topics), whole),
-            pl.BlockSpec((step, topics), part),
-            pl.BlockSpec((block, topics), whole),
-            pl.BlockSpec((topics, topics), whole),
+        in_specs=[hbm, vmem, hbm, vmem, vmem],
+        out_specs=(hbm, vmem, vmem),
+        scratch_shapes=[
+            pltpu.VMEM((rows, width), BF),
+            pltpu.VMEM((rows, topics), F32),
+            pltpu.VMEM((rows, topics), F32),
+            dma((parts,)), dma((parts,)), dma((parts,)),
         ],
-        out_specs=(
-            pl.BlockSpec((step, topics), part),
-            pl.BlockSpec((block, topics), whole),
-            pl.BlockSpec((topics, topics), whole),
-        ),
         compiler_params=pltpu.CompilerParams(vmem_limit_bytes=62 * 1024 * 1024),
         name="statistic",
     )(tile_values, weights, data_stat, codes_t, gram)

time: 137 us -> 129 us (0.942); the launches traced: 135 us -> 129 us
  Pallas kernels: 135 us -> 129 us
    pallas_call x1, Pallas kernels: 127 us -> 122 us  [per_device(): pl.pallas_call(functools.partial(codes_kernel, n), out_shape=(jax.ShapeDt...]
where the time goes in v4:
time: 129 us
  Pallas kernels  129 us (100%)
    pallas_call x1, Pallas kernels, per_device(): pl.pallas_call(functools.partial(codes_kernel, n), out_shape=(jax.ShapeDt...  122 us
    pallas_call x1, Pallas kernels, per_device(): pl.pallas_call(functools.partial(statistic_kernel, parts), out_shape=(jax...  6.77 us

profile of v4, /device:TPU:1, one launch (start us, length us, event | category | flops | bytes accessed | tf_op | source)
XLA Modules:
  0.0 129.3 jit_solution(1960996674152560288)
XLA Ops:
  0.6 121.9 %codes.1 = (f32[16,128]{1,0:T(8,128)}, f32[128,128]{1,0:T(8,128)}, bf16[256,128]{1,0:T(8,128)(2,1)}) custom-call(bf16[8192,128]{1,0:T(8,128)(2,1)} %factor.1, bf16[8192,128]{1,0:T(8,128)(2,1)} %tiles.3, s32[1,128]{1,0:T(1,128)} %docs_in.1, f32[16,128]{1,0:T(8,128)} %bitcast.2, f32[128,128]{1,0:T(8,128)} %gram_stat_in.1), custom_call_target="tpu_custom_call" | custom-call | tf_op jit(solution)/shard_map/codes/pallas_call | solution.py:567
  122.5 6.8 %statistic.1 = (f32[8192,128]{1,0:T(8,128)}, f32[16,128]{1,0:T(8,128)}, f32[128,128]{1,0:T(8,128)}) custom-call(bf16[8192,128]{1,0:T(8,128)(2,1)} %tiles.3, bf16[256,128]{1,0:T(8,128)(2,1)} %get-tuple-element.9.weights, f32[8192,128]{1,0:T(8,128)} %stat.1, f32[16,128]{1,0:T(8,128)} %get-tuple-element.10.codes, f32[128,128]{1,0:T(8,128)} %get-tuple-element.11.gram), custom_call_target="tpu_custom_call" | custom-call | tf_op jit(solution)/shard_map/statistic/pallas_call | solution.py:612

commit v5 on v4

--- a/solution.py
+++ b/solution.py
@@ -12,7 +12,7 @@
 DECAY = 0.5
 PARTS = 4
 LAG_Y = 3
-LAG_X = 6
+LAG_X = 7
 HOLD = 10
 MESH = pl.DeviceIdType.MESH
 BF = jnp.bfloat16

time: 129 us -> 129 us (level)
  no operation moved by 1% of the time
where the time goes in v5:
time: 129 us
  Pallas kernels  128 us (99%)
    pallas_call x1, Pallas kernels, per_device(): pl.pallas_call(functools.partial(codes_kernel, n), out_shape=(jax.ShapeDt...  121 us
    pallas_call x1, Pallas kernels, per_device(): pl.pallas_call(functools.partial(statistic_kernel, parts), out_shape=(jax...  6.77 us

profile of v5, /device:TPU:1, one launch (start us, length us, event | category | flops | bytes accessed | tf_op | source)
XLA Modules:
  0.0 128.5 jit_solution(1711297070607767395)
XLA Ops:
  0.6 121.1 %codes.1 = (f32[16,128]{1,0:T(8,128)}, f32[128,128]{1,0:T(8,128)}, bf16[256,128]{1,0:T(8,128)(2,1)}) custom-call(bf16[8192,128]{1,0:T(8,128)(2,1)} %factor.1, bf16[8192,128]{1,0:T(8,128)(2,1)} %tiles.3, s32[1,128]{1,0:T(1,128)} %docs_in.1, f32[16,128]{1,0:T(8,128)} %bitcast.2, f32[128,128]{1,0:T(8,128)} %gram_stat_in.1), custom_call_target="tpu_custom_call" | custom-call | tf_op jit(solution)/shard_map/codes/pallas_call | solution.py:567
  121.8 6.8 %statistic.1 = (f32[8192,128]{1,0:T(8,128)}, f32[16,128]{1,0:T(8,128)}, f32[128,128]{1,0:T(8,128)}) custom-call(bf16[8192,128]{1,0:T(8,128)(2,1)} %tiles.3, bf16[256,128]{1,0:T(8,128)(2,1)} %get-tuple-element.9.weights, f32[8192,128]{1,0:T(8,128)} %stat.1, f32[16,128]{1,0:T(8,128)} %get-tuple-element.10.codes, f32[128,128]{1,0:T(8,128)} %get-tuple-element.11.gram), custom_call_target="tpu_custom_call" | custom-call | tf_op jit(solution)/shard_map/statistic/pallas_call | solution.py:612

commit v6 on v5

--- a/solution.py
+++ b/solution.py
@@ -520,7 +520,7 @@
 
 def statistic_kernel(
     parts, tiles, weights, stat, codes, gram, out, codes_out, gram_out,
-    tiles_v, stat_v, out_v, tile_sem, stat_sem, out_sem,
+    tiles_v, stat_v, out_v, weights_v, tile_sem, stat_sem, out_sem, small_sem,
 ):
     rows = tiles.shape[0] // parts
 
@@ -535,22 +535,30 @@
         where = pl.ds(s * rows, rows)
         return pltpu.make_async_copy(out_v.at[where], out.at[where], out_sem.at[s])
 
+    small = [
+        pltpu.make_async_copy(a, b, small_sem.at[s])
+        for s, (a, b) in enumerate([(weights, weights_v), (codes, codes_out), (gram, gram_out)])
+    ]
+    small[0].start()
     for s in range(parts):
         for copy in load(s):
             copy.start()
-    codes_out[...] = codes[...]
-    gram_out[...] = gram[...]
+    small[1].start()
+    small[2].start()
+    small[0].wait()
     for s in range(parts):
         for copy in load(s):
             copy.wait()
         where = pl.ds(s * rows, rows)
         part = tiles_v[where, :]
         out_v[where, :] = DECAY * stat_v[where, :] + dot(
-            jnp.concatenate([part, part], axis=1), weights[...]
+            jnp.concatenate([part, part], axis=1), weights_v[...]
         )
         store(s).start()
     for s in range(parts):
         store(s).wait()
+    small[1].wait()
+    small[2].wait()
 
 
 def per_device(n, factor, tile_values, tile_docs, codes, gram_stat, data_stat):
@@ -616,13 +624,14 @@
             jax.ShapeDtypeStruct((block, topics), F32),
             jax.ShapeDtypeStruct((topics, topics), F32),
         ),
-        in_specs=[hbm, vmem, hbm, vmem, vmem],
-        out_specs=(hbm, vmem, vmem),
+        in_specs=[hbm] * 5,
+        out_specs=(hbm, hbm, hbm),
         scratch_shapes=[
             pltpu.VMEM((rows, width), BF),
             pltpu.VMEM((rows, topics), F32),
             pltpu.VMEM((rows, topics), F32),
-            dma((parts,)), dma((parts,)), dma((parts,)),
+            pltpu.VMEM((2 * width, topics), BF),
+            dma((parts,)), dma((parts,)), dma((parts,)), dma((3,)),
         ],
         compiler_params=pltpu.CompilerParams(vmem_limit_bytes=62 * 1024 * 1024),
         name="statistic",

time: 129 us -> 128 us (level)
  no operation moved by 1% of the time
where the time goes in v6:
time: 128 us
  Pallas kernels  127 us (99%)
    pallas_call x1, Pallas kernels, per_device(): pl.pallas_call(functools.partial(codes_kernel, n), out_shape=(jax.ShapeDt...  121 us
    pallas_call x1, Pallas kernels, per_device(): pl.pallas_call(functools.partial(statistic_kernel, parts), out_shape=(jax...  6.17 us

profile of v6, /device:TPU:1, one launch (start us, length us, event | category | flops | bytes accessed | tf_op | source)
XLA Modules:
  0.0 128.0 jit_solution(10708391257809114043)
XLA Ops:
  0.6 121.1 %codes.1 = (f32[16,128]{1,0:T(8,128)}, f32[128,128]{1,0:T(8,128)}, bf16[256,128]{1,0:T(8,128)(2,1)}) custom-call(bf16[8192,128]{1,0:T(8,128)(2,1)} %factor.1, bf16[8192,128]{1,0:T(8,128)(2,1)} %tiles.3, s32[1,128]{1,0:T(1,128)} %docs_in.1, f32[16,128]{1,0:T(8,128)} %bitcast.2, f32[128,128]{1,0:T(8,128)} %gram_stat_in.1), custom_call_target="tpu_custom_call" | custom-call | tf_op jit(solution)/shard_map/codes/pallas_call | solution.py:575
  121.8 6.2 %statistic.1 = (f32[8192,128]{1,0:T(8,128)}, f32[16,128]{1,0:T(8,128)}, f32[128,128]{1,0:T(8,128)}) custom-call(bf16[8192,128]{1,0:T(8,128)(2,1)} %tiles.3, bf16[256,128]{1,0:T(8,128)(2,1)} %get-tuple-element.9.weights, f32[8192,128]{1,0:T(8,128)} %stat.1, f32[16,128]{1,0:T(8,128)} %get-tuple-element.10.codes, f32[128,128]{1,0:T(8,128)} %get-tuple-element.11.gram), custom_call_target="tpu_custom_call" | custom-call | tf_op jit(solution)/shard_map/statistic/pallas_call | solution.py:620
